TPU v7x, 32 devices: a whole 2x2x4 slice. The times are simulated.
32 devices in a mesh: fsdp: 16 (over z, y, x), seq: 2 (over core).
Axes of the slice: x: 2, y: 2, z: 4, core: 2. Of those that a mesh axis runs over, the one named last changes fastest.
Arguments:
- tokens: bfloat16 [32, 1024, 1152], P('fsdp', 'seq'), may hold values from -6 to 6
- timestep: bfloat16 [32, 6912], P('fsdp'), may hold values from -1.5 to 1.5
- text: bfloat16 [32, 120, 1152], P('fsdp', 'seq'), may hold values from -6 to 6
- cotangent: bfloat16 [32, 1024, 1152], P('fsdp', 'seq'), may hold values from -6 to 6
- vectors: bfloat16 [1152, 17], P('fsdp'), may hold values from -1.5 to 1.5
- w_qkv: bfloat16 [1152, 3456], P('fsdp', 'seq'), may hold values from -0.1875 to 0.1875
- w_out: bfloat16 [1152, 1152], P('fsdp', 'seq'), may hold values from -0.5 to 0.5
- w_query2: bfloat16 [1152, 1152], P('fsdp', 'seq'), may hold values from -0.1875 to 0.1875
- w_kv2: bfloat16 [1152, 2304], P('fsdp', 'seq'), may hold values from -0.1875 to 0.1875
- w_out2: bfloat16 [1152, 1152], P('fsdp', 'seq'), may hold values from -0.375 to 0.375
- w_fc1: bfloat16 [1152, 4608], P('fsdp', 'seq'), may hold values from -0.1875 to 0.1875
- w_fc2: bfloat16 [4608, 1152], P('fsdp', 'seq'), may hold values from -0.125 to 0.125
Outputs:
- result: bfloat16 [32, 1024, 1152], P('fsdp', 'seq')
- grad_tokens: float32 [32, 1024, 1152], P('fsdp', 'seq')
- grad_timestep: float32 [32, 6912], P('fsdp')
- grad_text: float32 [32, 120, 1152], P('fsdp', 'seq')
- grad_vectors: float32 [1152, 17], P('fsdp')
- grad_qkv: float32 [1152, 3456], P('fsdp', 'seq')
- grad_out: float32 [1152, 1152], P('fsdp', 'seq')
- grad_query2: float32 [1152, 1152], P('fsdp', 'seq')
- grad_kv2: float32 [1152, 2304], P('fsdp', 'seq')
- grad_out2: float32 [1152, 1152], P('fsdp', 'seq')
- grad_fc1: float32 [1152, 4608], P('fsdp', 'seq')
- grad_fc2: float32 [4608, 1152], P('fsdp', 'seq')
All inputs are finite; a program needn't handle non-finite values.
Results may differ from a plain program's by a relative error of at most 0.015.
Values may be sent and summed in bfloat16 or wider, within the bound.
No kernel may reach another device: no remote copies, remote signals or barrier semaphores. Data moves between devices by JAX's collectives and lax.ppermute only.
A program may use at most 512 MiB of HBM per device.

v0:
```python
import jax
import jax.numpy as jnp
from jax import lax
from jax.sharding import PartitionSpec as P

D = 1152
HEADS = 16
HEAD_DIM = 72
MICRO = 2


norm_eps = 1e-06
gelu_root = 0.7978845608028654
gelu_cube = 0.044715


def norm_rows(inputs):
    center = inputs - jnp.mean(inputs, axis=-1, keepdims=True)
    spread = jnp.mean(center * center, axis=-1, keepdims=True)
    return center * lax.rsqrt(spread + norm_eps)


def gelu_tanh(inputs):
    return (
        0.5 * inputs * (1.0 + jnp.tanh(gelu_root * (inputs + gelu_cube * inputs * inputs * inputs)))
    )


def modulated(inputs, shift_rows, scale_rows):
    return norm_rows(inputs) * (1.0 + scale_rows) + shift_rows


def flatten(tensor):
    return tensor.reshape(-1, tensor.shape[-1])


def split_heads(tensor):
    return tensor.reshape(tensor.shape[0], tensor.shape[1], HEADS, HEAD_DIM)


def attend_forward(queries, key_rows, value_rows):
    scale_factor = HEAD_DIM ** (-0.5)
    scores = (
        jnp.einsum(
            "bqhd,bkhd->bhqk",
            split_heads(queries),
            split_heads(key_rows),
            preferred_element_type=jnp.float32,
        )
        * scale_factor
    )
    row_top = jnp.max(scores, axis=-1, keepdims=True)
    exponent = jnp.exp(scores - row_top)
    totals = jnp.sum(exponent, axis=-1, keepdims=True)
    attn_weights = (exponent / totals).astype(jnp.bfloat16)
    mixed = jnp.einsum(
        "bhqk,bkhd->bqhd", attn_weights, split_heads(value_rows), preferred_element_type=jnp.float32
    )
    return (mixed.reshape(queries.shape), row_top + jnp.log(totals))


def attend_backward(queries, key_rows, value_rows, log_totals, grad_mixed):
    scale_factor = HEAD_DIM ** (-0.5)
    q_heads = split_heads(queries)
    k_heads = split_heads(key_rows)
    g_heads = split_heads(grad_mixed)
    scores = (
        jnp.einsum("bqhd,bkhd->bhqk", q_heads, k_heads, preferred_element_type=jnp.float32)
        * scale_factor
    )
    attn_weights = jnp.exp(scores - log_totals)
    grad_weights = jnp.einsum(
        "bqhd,bkhd->bhqk", g_heads, split_heads(value_rows), preferred_element_type=jnp.float32
    )
    row_dot = jnp.sum(grad_weights * attn_weights, axis=-1, keepdims=True)
    grad_scores = (attn_weights * (grad_weights - row_dot)).astype(jnp.bfloat16)
    grad_queries = (
        jnp.einsum("bhqk,bkhd->bqhd", grad_scores, k_heads, preferred_element_type=jnp.float32)
        * scale_factor
    )
    grad_keys = (
        jnp.einsum("bhqk,bqhd->bkhd", grad_scores, q_heads, preferred_element_type=jnp.float32)
        * scale_factor
    )
    grad_values = jnp.einsum(
        "bhqk,bqhd->bkhd",
        attn_weights.astype(jnp.bfloat16),
        g_heads,
        preferred_element_type=jnp.float32,
    )
    return (
        grad_queries.reshape(queries.shape),
        grad_keys.reshape(key_rows.shape),
        grad_values.reshape(value_rows.shape),
    )


def layer_forward(weights, token_rows, time_rows, text_rows):
    w_qkv, w_out, w_query2, w_kv2, w_out2, w_fc1, w_fc2, vec_cols = weights
    image_count = token_rows.shape[0]
    token_count = token_rows.shape[1]
    inputs = token_rows.astype(jnp.float32)
    modulation = vec_cols[:, :6].astype(jnp.float32).T[None] + time_rows.astype(
        jnp.float32
    ).reshape(image_count, 6, D)
    vec_float = vec_cols.astype(jnp.float32)
    zero_bias = jnp.zeros((D,), jnp.float32)
    h_attn = modulated(inputs, modulation[:, 0:1], modulation[:, 1:2]).astype(jnp.bfloat16)
    qkv_bias = jnp.concatenate([vec_float[:, 6], zero_bias, vec_float[:, 7]])
    qkv_rows = (
        jnp.dot(flatten(h_attn), w_qkv, preferred_element_type=jnp.float32) + qkv_bias
    ).astype(jnp.bfloat16)
    qkv_rows = qkv_rows.reshape(image_count, token_count, 3 * D)
    self_query = qkv_rows[..., :D]
    all_keys, all_values = (
        lax.all_gather(qkv_rows[..., D : 2 * D], "seq", axis=1, tiled=True),
        lax.all_gather(qkv_rows[..., 2 * D :], "seq", axis=1, tiled=True),
    )
    attn_mixed, self_lse = attend_forward(self_query, all_keys, all_values)
    attn_low = attn_mixed.astype(jnp.bfloat16)
    attn_proj = (
        jnp.dot(flatten(attn_low), w_out, preferred_element_type=jnp.float32) + vec_float[:, 8]
    ).reshape(image_count, token_count, D)
    after_attn = inputs + modulation[:, 2:3] * attn_proj
    after_low = after_attn.astype(jnp.bfloat16)
    cross_query = (
        jnp.dot(flatten(after_low), w_query2, preferred_element_type=jnp.float32) + vec_float[:, 9]
    ).astype(jnp.bfloat16)
    cross_query = cross_query.reshape(image_count, token_count, D)
    kv_bias = jnp.concatenate([zero_bias, vec_float[:, 10]])
    text_kv = (
        jnp.dot(flatten(text_rows), w_kv2, preferred_element_type=jnp.float32) + kv_bias
    ).astype(jnp.bfloat16)
    text_kv = text_kv.reshape(image_count, text_rows.shape[1], 2 * D)
    text_keys, text_values = (
        lax.all_gather(text_kv[..., :D], "seq", axis=1, tiled=True),
        lax.all_gather(text_kv[..., D:], "seq", axis=1, tiled=True),
    )
    cross_mixed, cross_lse = attend_forward(cross_query, text_keys, text_values)
    cross_low = cross_mixed.astype(jnp.bfloat16)
    cross_proj = (
        jnp.dot(flatten(cross_low), w_out2, preferred_element_type=jnp.float32) + vec_float[:, 11]
    )
    after_cross = after_attn + cross_proj.reshape(image_count, token_count, D)
    h_mlp = modulated(after_cross, modulation[:, 3:4], modulation[:, 4:5]).astype(jnp.bfloat16)
    fc1_bias = vec_float[:, 13:].T.reshape(-1)
    hidden_pre = jnp.dot(flatten(h_mlp), w_fc1, preferred_element_type=jnp.float32) + fc1_bias
    hidden_low = gelu_tanh(hidden_pre).astype(jnp.bfloat16)
    mlp_out = (
        jnp.dot(hidden_low, w_fc2, preferred_element_type=jnp.float32) + vec_float[:, 12]
    ).reshape(image_count, token_count, D)
    result = (after_cross + modulation[:, 5:6] * mlp_out).astype(jnp.bfloat16)
    saved_state = (
        inputs,
        modulation,
        h_attn,
        self_query,
        all_keys,
        all_values,
        self_lse,
        attn_low,
        attn_proj,
        after_attn,
        after_low,
        cross_query,
        text_keys,
        text_values,
        cross_lse,
        cross_low,
        after_cross,
        h_mlp,
        hidden_pre,
        hidden_low,
        mlp_out,
        text_rows,
    )
    return (result, saved_state)


def layer_backward(weights, saved_state, grad_result):
    w_qkv, w_out, w_query2, w_kv2, w_out2, w_fc1, w_fc2, vec_cols = weights
    (
        inputs,
        modulation,
        h_attn,
        self_query,
        all_keys,
        all_values,
        self_lse,
        attn_low,
        attn_proj,
        after_attn,
        after_low,
        cross_query,
        text_keys,
        text_values,
        cross_lse,
        cross_low,
        after_cross,
        h_mlp,
        hidden_pre,
        hidden_low,
        mlp_out,
        text_rows,
    ) = saved_state
    image_count = grad_result.shape[0]
    token_count = grad_result.shape[1]
    grad_gate_mlp = jnp.sum(grad_result * mlp_out, axis=1, keepdims=True)
    grad_mlp = flatten(modulation[:, 5:6] * grad_result).astype(jnp.bfloat16)
    fc2_grad = jnp.einsum("rf,rd->fd", hidden_low, grad_mlp, preferred_element_type=jnp.float32)
    fc2_bias = jnp.sum(grad_mlp.astype(jnp.float32), axis=0)
    grad_hidden = jnp.einsum("rd,fd->rf", grad_mlp, w_fc2, preferred_element_type=jnp.float32)
    grad_pre = jax.vjp(gelu_tanh, hidden_pre)[1](grad_hidden)[0].astype(jnp.bfloat16)
    fc1_grad = jnp.einsum("rd,rf->df", flatten(h_mlp), grad_pre, preferred_element_type=jnp.float32)
    fc1_bias = jnp.sum(grad_pre.astype(jnp.float32), axis=0)
    grad_h_mlp = jnp.einsum(
        "rf,df->rd", grad_pre, w_fc1, preferred_element_type=jnp.float32
    ).reshape(image_count, token_count, D)
    mlp_pull = jax.vjp(modulated, after_cross, modulation[:, 3:4], modulation[:, 4:5])[1]
    grad_cross, grad_shift_mlp, grad_scale_mlp = mlp_pull(grad_h_mlp)
    grad_cross = grad_cross + grad_result
    grad_proj2 = flatten(grad_cross).astype(jnp.bfloat16)
    out2_grad = jnp.einsum(
        "rd,re->de", flatten(cross_low), grad_proj2, preferred_element_type=jnp.float32
    )
    out2_bias = jnp.sum(grad_proj2.astype(jnp.float32), axis=0)
    grad_mixed2 = jnp.einsum(
        "re,de->rd", grad_proj2, w_out2, preferred_element_type=jnp.float32
    ).astype(jnp.bfloat16)
    grad_mixed2 = grad_mixed2.reshape(image_count, token_count, D)
    grad_q2, grad_k2, grad_v2 = attend_backward(
        cross_query, text_keys, text_values, cross_lse, grad_mixed2
    )
    own_k2, own_v2 = (
        lax.psum_scatter(grad_k2, "seq", scatter_dimension=1, tiled=True),
        lax.psum_scatter(grad_v2, "seq", scatter_dimension=1, tiled=True),
    )
    grad_kv = flatten(jnp.concatenate([own_k2, own_v2], axis=-1).astype(jnp.bfloat16))
    kv2_grad = jnp.einsum(
        "rd,re->de", flatten(text_rows), grad_kv, preferred_element_type=jnp.float32
    )
    kv2_bias = jnp.sum(grad_kv[:, D:].astype(jnp.float32), axis=0)
    grad_text = jnp.einsum("re,de->rd", grad_kv, w_kv2, preferred_element_type=jnp.float32).reshape(
        image_count, own_k2.shape[1], D
    )
    grad_q2_low = flatten(grad_q2).astype(jnp.bfloat16)
    query2_grad = jnp.einsum(
        "rd,re->de", flatten(after_low), grad_q2_low, preferred_element_type=jnp.float32
    )
    query2_bias = jnp.sum(grad_q2_low.astype(jnp.float32), axis=0)
    grad_attn = grad_cross + jnp.einsum(
        "re,de->rd", grad_q2_low, w_query2, preferred_element_type=jnp.float32
    ).reshape(image_count, token_count, D)
    grad_gate_attn = jnp.sum(grad_attn * attn_proj, axis=1, keepdims=True)
    grad_proj1 = flatten(modulation[:, 2:3] * grad_attn).astype(jnp.bfloat16)
    out_grad = jnp.einsum(
        "rd,re->de", flatten(attn_low), grad_proj1, preferred_element_type=jnp.float32
    )
    out_bias = jnp.sum(grad_proj1.astype(jnp.float32), axis=0)
    grad_mixed1 = jnp.einsum(
        "re,de->rd", grad_proj1, w_out, preferred_element_type=jnp.float32
    ).astype(jnp.bfloat16)
    grad_mixed1 = grad_mixed1.reshape(image_count, token_count, D)
    grad_q1, grad_k1, grad_v1 = attend_backward(
        self_query, all_keys, all_values, self_lse, grad_mixed1
    )
    own_k1, own_v1 = (
        lax.psum_scatter(grad_k1, "seq", scatter_dimension=1, tiled=True),
        lax.psum_scatter(grad_v1, "seq", scatter_dimension=1, tiled=True),
    )
    grad_qkv = flatten(jnp.concatenate([grad_q1, own_k1, own_v1], axis=-1).astype(jnp.bfloat16))
    qkv_grad = jnp.einsum(
        "rd,re->de", flatten(h_attn), grad_qkv, preferred_element_type=jnp.float32
    )
    qkv_sums = jnp.sum(grad_qkv.astype(jnp.float32), axis=0)
    grad_h_attn = jnp.einsum(
        "re,de->rd", grad_qkv, w_qkv, preferred_element_type=jnp.float32
    ).reshape(image_count, token_count, D)
    attn_pull = jax.vjp(modulated, inputs, modulation[:, 0:1], modulation[:, 1:2])[1]
    grad_inputs, grad_shift_attn, grad_scale_attn = attn_pull(grad_h_attn)
    grad_inputs = grad_inputs + grad_attn
    grad_modulation = jnp.concatenate(
        [
            grad_shift_attn,
            grad_scale_attn,
            grad_gate_attn,
            grad_shift_mlp,
            grad_scale_mlp,
            grad_gate_mlp,
        ],
        axis=1,
    )
    bias_cols = jnp.stack(
        [qkv_sums[:D], qkv_sums[2 * D :], out_bias, query2_bias, kv2_bias, out2_bias, fc2_bias],
        axis=1,
    )
    vec_grad = jnp.concatenate(
        [jnp.sum(grad_modulation, axis=0).T, bias_cols, fc1_bias.reshape(-1, D).T], axis=1
    )
    grad_terms = (
        qkv_grad,
        out_grad,
        query2_grad,
        kv2_grad,
        out2_grad,
        fc1_grad,
        fc2_grad,
        vec_grad,
    )
    return (grad_inputs, grad_modulation.reshape(image_count, 6 * D), grad_text, grad_terms)


def body(
    tokens, timestep, text, cotangent, vectors, w_qkv, w_out, w_query2, w_kv2, w_out2, w_fc1, w_fc2
):

    def gather_weights():
        col_parts = (
            lax.all_gather(w_qkv, "seq", axis=1, tiled=True),
            lax.all_gather(w_out, "seq", axis=1, tiled=True),
            lax.all_gather(w_query2, "seq", axis=1, tiled=True),
            lax.all_gather(w_kv2, "seq", axis=1, tiled=True),
            lax.all_gather(w_out2, "seq", axis=1, tiled=True),
            lax.all_gather(w_fc1, "seq", axis=1, tiled=True),
            lax.all_gather(w_fc2, "seq", axis=1, tiled=True),
        )
        return (
            lax.all_gather(col_parts[0], "fsdp", axis=0, tiled=True),
            lax.all_gather(col_parts[1], "fsdp", axis=0, tiled=True),
            lax.all_gather(col_parts[2], "fsdp", axis=0, tiled=True),
            lax.all_gather(col_parts[3], "fsdp", axis=0, tiled=True),
            lax.all_gather(col_parts[4], "fsdp", axis=0, tiled=True),
            lax.all_gather(col_parts[5], "fsdp", axis=0, tiled=True),
            lax.all_gather(col_parts[6], "fsdp", axis=0, tiled=True),
            lax.all_gather(vectors, "fsdp", axis=0, tiled=True),
        )

    per_micro = tokens.shape[0] // MICRO
    results = []
    token_grads = []
    time_grads = []
    text_grads = []
    shard_sums = None
    for micro_step in range(MICRO):
        first_row = micro_step * per_micro
        last_row = first_row + per_micro
        weights = gather_weights()
        result, saved_state = layer_forward(
            weights,
            tokens[first_row:last_row],
            timestep[first_row:last_row],
            text[first_row:last_row],
        )
        weights = gather_weights()
        grad_inputs, grad_time, grad_text, grad_terms = layer_backward(
            weights, saved_state, cotangent[first_row:last_row].astype(jnp.float32)
        )
        shards = (
            lax.psum_scatter(
                lax.psum_scatter(grad_terms[0], "fsdp", scatter_dimension=0, tiled=True),
                "seq",
                scatter_dimension=1,
                tiled=True,
            ),
            lax.psum_scatter(
                lax.psum_scatter(grad_terms[1], "fsdp", scatter_dimension=0, tiled=True),
                "seq",
                scatter_dimension=1,
                tiled=True,
            ),
            lax.psum_scatter(
                lax.psum_scatter(grad_terms[2], "fsdp", scatter_dimension=0, tiled=True),
                "seq",
                scatter_dimension=1,
                tiled=True,
            ),
            lax.psum_scatter(
                lax.psum_scatter(grad_terms[3], "fsdp", scatter_dimension=0, tiled=True),
                "seq",
                scatter_dimension=1,
                tiled=True,
            ),
            lax.psum_scatter(
                lax.psum_scatter(grad_terms[4], "fsdp", scatter_dimension=0, tiled=True),
                "seq",
                scatter_dimension=1,
                tiled=True,
            ),
            lax.psum_scatter(
                lax.psum_scatter(grad_terms[5], "fsdp", scatter_dimension=0, tiled=True),
                "seq",
                scatter_dimension=1,
                tiled=True,
            ),
            lax.psum_scatter(
                lax.psum_scatter(grad_terms[6], "fsdp", scatter_dimension=0, tiled=True),
                "seq",
                scatter_dimension=1,
                tiled=True,
            ),
            lax.psum_scatter(grad_terms[7], "fsdp", scatter_dimension=0, tiled=True),
        )
        shard_sums = shards if micro_step == 0 else jax.tree.map(jnp.add, shard_sums, shards)
        results.append(result)
        token_grads.append(grad_inputs)
        time_grads.append(grad_time)
        text_grads.append(grad_text)
    vec_total, time_total = lax.psum((shard_sums[7], jnp.concatenate(time_grads, axis=0)), "seq")
    return (
        jnp.concatenate(results, axis=0),
        jnp.concatenate(token_grads, axis=0),
        time_total,
        jnp.concatenate(text_grads, axis=0),
        vec_total,
        shard_sums[0],
        shard_sums[1],
        shard_sums[2],
        shard_sums[3],
        shard_sums[4],
        shard_sums[5],
        shard_sums[6],
    )


def solution(mesh):
    in_specs = (
        P("fsdp", "seq", None),
        P("fsdp", None),
        P("fsdp", "seq", None),
        P("fsdp", "seq", None),
        P("fsdp", None),
        P("fsdp", "seq"),
        P("fsdp", "seq"),
        P("fsdp", "seq"),
        P("fsdp", "seq"),
        P("fsdp", "seq"),
        P("fsdp", "seq"),
        P("fsdp", "seq"),
    )
    out_specs = (
        P("fsdp", "seq", None),
        P("fsdp", "seq", None),
        P("fsdp", None),
        P("fsdp", "seq", None),
        P("fsdp", None),
        P("fsdp", "seq"),
        P("fsdp", "seq"),
        P("fsdp", "seq"),
        P("fsdp", "seq"),
        P("fsdp", "seq"),
        P("fsdp", "seq"),
        P("fsdp", "seq"),
    )
    return jax.shard_map(body, mesh=mesh, in_specs=in_specs, out_specs=out_specs, check_vma=False)
```

profile of v0, /device:TPU:0, one launch (start us, length us, event | category | flops | bytes accessed | tf_op | source)
XLA Modules:
  0.0 2988.3 jit_solution(4544854686684623928)
XLA Ops:
  13.8 43.4 %all-gather = bf16[16,72,17]{1,2,0:T(8,128)(2,1)S(1)} all-gather(bf16[1,72,17]{1,2,0:T(8,128)(2,1)S(1)} %bitcast.547), channel_id=1, replica_groups=mesh['fsdp'=16,'seq'=2] {'fsdp'}, dimensions={0}, use_global_device_ids=true | all-gather | bytes 41616 | tf_op jit(solution)/shard_map/all_gather | solution.py:335
  59.7 64.0 %all-gather.18.cloned.1.call-done = bf16[1152,3456]{1,0:T(8,128)(2,1)} async-done(((bf16[72,3456]{1,0:T(8,128)(2,1)}), bf16[1152,3456]{1,0:T(8,128)(2,1)}) %all-gather.18.cloned.1.call-update) | async-done | bytes 7962640 | tf_op jit(solution)/shard_map/all_gather | solution.py:328
  153.3 57.0 %all-gather.26.cloned.1.call-done = bf16[1152,2304]{1,0:T(8,128)(2,1)} async-done(((bf16[72,2304]{1,0:T(8,128)(2,1)}), bf16[1152,2304]{1,0:T(8,128)(2,1)}) %all-gather.26.cloned.1.call-update) | async-done | bytes 5308432 | tf_op jit(solution)/shard_map/all_gather | solution.py:331
  239.8 15.2 multiply_reduce_fusion.3
  283.5 20.6 all-gather.24.cloned.1.call-done
  309.5 61.0 %all-gather.28.cloned.1.call-done = bf16[1152,1152]{1,0:T(8,128)(2,1)} async-done(((bf16[72,1152]{1,0:T(8,128)(2,1)}), bf16[1152,1152]{1,0:T(8,128)(2,1)}) %all-gather.28.cloned.1.call-update) | async-done | bytes 2654224 | tf_op jit(solution)/shard_map/all_gather | solution.py:330
  381.9 55.1 %all-gather.30.cloned.1.call-done = bf16[1152,1152]{1,0:T(8,128)(2,1)} async-done(((bf16[72,1152]{1,0:T(8,128)(2,1)}), bf16[1152,1152]{1,0:T(8,128)(2,1)}) %all-gather.30.cloned.1.call-update) | async-done | bytes 2654224 | tf_op jit(solution)/shard_map/all_gather | solution.py:332
  444.8 127.4 %all-gather.32.cloned.1.call-done = bf16[1152,4608]{1,0:T(8,128)(2,1)} async-done(((bf16[72,4608]{1,0:T(8,128)(2,1)}), bf16[1152,4608]{1,0:T(8,128)(2,1)}) %all-gather.32.cloned.1.call-update) | async-done | bytes 10616848 | tf_op jit(solution)/shard_map/all_gather | solution.py:333
  584.6 122.7 %all-gather.34.cloned.1.call-done = bf16[4608,1152]{1,0:T(8,128)(2,1)} async-done(((bf16[288,1152]{1,0:T(8,128)(2,1)}), bf16[4608,1152]{1,0:T(8,128)(2,1)}) %all-gather.34.cloned.1.call-update) | async-done | bytes 10616848 | tf_op jit(solution)/shard_map/all_gather | solution.py:334
  707.3 18.4 convert_reduce_fusion.1
  766.4 23.3 multiply_reduce_fusion.1
  789.7 28.5 multiply_convert_fusion.1
  829.9 17.3 fusion.6
  907.3 15.2 multiply_reduce_fusion.2
  984.8 18.0 convert_reduce_fusion
  1031.2 15.6 fusion.68
  1072.2 23.3 multiply_reduce_fusion
  1095.5 28.5 multiply_convert_fusion
  1135.8 17.3 fusion.4
  1183.1 25.7 all-reduce.17
  1314.1 63.4 %all-reduce.16.cloned.1.call-done = f32[1152,17]{0,1:T(8,128)} async-done(((f32[1152,17]{0,1:T(8,128)}), f32[1152,17]{0,1:T(8,128)}) %all-reduce.16.cloned.1.call-update) | async-done | bytes 78352
  1379.0 26.4 all-reduce.18
  1442.0 14.8 convolution_add_fusion.2
  1458.4 14.8 fusion.109
  1473.2 18.7 convolution_add_fusion
  1505.6 19.8 convolution_add_fusion.1
  1527.5 140.8 %reduce-scatter.72.cloned.1.call-done = f32[72,1152]{1,0:T(8,128)} async-done(((f32[1152,1152]{1,0:T(8,128)}), f32[72,1152]{1,0:T(8,128)}) %reduce-scatter.72.cloned.1.call-update) | async-done | bytes 331792
  1670.4 143.4 %reduce-scatter.70.cloned.1.call-done = f32[72,1152]{1,0:T(8,128)} async-done(((f32[1152,1152]{1,0:T(8,128)}), f32[72,1152]{1,0:T(8,128)}) %reduce-scatter.70.cloned.1.call-update) | async-done | bytes 331792
  1815.9 184.8 %reduce-scatter.66.cloned.1.call-done = f32[72,2304]{1,0:T(8,128)} async-done(((f32[1152,2304]{1,0:T(8,128)}), f32[72,2304]{1,0:T(8,128)}) %reduce-scatter.66.cloned.1.call-update) | async-done | bytes 663568
  2003.3 255.9 %reduce-scatter.68.cloned.1.call-done = f32[72,3456]{1,0:T(8,128)} async-done(((f32[1152,3456]{1,0:T(8,128)}), f32[72,3456]{1,0:T(8,128)}) %reduce-scatter.68.cloned.1.call-update) | async-done | bytes 995344
  2262.3 317.3 %reduce-scatter.54.cloned.1.call-done = f32[288,1152]{1,0:T(8,128)} async-done(((f32[4608,1152]{1,0:T(8,128)}), f32[288,1152]{1,0:T(8,128)}) %reduce-scatter.54.cloned.1.call-update) | async-done | bytes 1327120 | tf_op jit(solution)/shard_map/reduce_scatter | solution.py:396
  2582.8 315.1 %reduce-scatter.52.cloned.1.call-done = f32[72,4608]{1,0:T(8,128)} async-done(((f32[1152,4608]{1,0:T(8,128)}), f32[72,4608]{1,0:T(8,128)}) %reduce-scatter.52.cloned.1.call-update) | async-done | bytes 1327120 | tf_op jit(solution)/shard_map/reduce_scatter | solution.py:390
  (739 shorter events, 656.8 us)
Async XLA Ops:
  7.2 116.5 %all-gather.18.cloned.1.call-start = ((), (), s32[]{:S(2)}) async-start(), calls=%async_computation.18 | async-start | bytes 8460288 | tf_op jit(solution)/shard_map/all_gather | solution.py:328
  11.4 198.9 %all-gather.26.cloned.1.call-start = ((), (), s32[]{:S(2)}) async-start(), calls=%async_computation.22 | async-start | bytes 5640192 | tf_op jit(solution)/shard_map/all_gather | solution.py:331
  13.7 209.1 %all-gather.22.cloned.1.call-start = ((), (), s32[]{:S(2)}) async-start(), calls=%async_computation.20 | async-start | bytes 3538944 | tf_op jit(solution)/shard_map/all_gather | solution.py:116
  134.4 101.2 %all-gather.20.cloned.1.call-start = ((), (), s32[]{:S(2)}) async-start(), calls=%async_computation.19 | async-start | bytes 3538944 | tf_op jit(solution)/shard_map/all_gather | solution.py:117
  134.9 169.2 %all-gather.24.cloned.1.call-start = ((), (), s32[]{:S(2)}) async-start(), calls=%async_computation.21 | async-start | bytes 2820096 | tf_op jit(solution)/shard_map/all_gather | solution.py:329
  138.1 232.3 %all-gather.28.cloned.1.call-start = ((), (), s32[]{:S(2)}) async-start(), calls=%async_computation.23 | async-start | bytes 2820096 | tf_op jit(solution)/shard_map/all_gather | solution.py:330
  141.3 295.6 %all-gather.30.cloned.1.call-start = ((), (), s32[]{:S(2)}) async-start(), calls=%async_computation.24 | async-start | bytes 2820096 | tf_op jit(solution)/shard_map/all_gather | solution.py:332
  144.5 427.7 %all-gather.32.cloned.1.call-start = ((), (), s32[]{:S(2)}) async-start(), calls=%async_computation.25 | async-start | bytes 11280384 | tf_op jit(solution)/shard_map/all_gather | solution.py:333
  147.1 560.2 %all-gather.34.cloned.1.call-start = ((), (), s32[]{:S(2)}) async-start(), calls=%async_computation.26 | async-start | bytes 11280384 | tf_op jit(solution)/shard_map/all_gather | solution.py:334
  151.5 710.1 %reduce-scatter.40.cloned.1.call-start = ((), (), s32[]{:S(2)}) async-start(), calls=%async_computation.29 | async-start | bytes 7077888 | tf_op jit(solution)/shard_map/reduce_scatter | solution.py:268
  829.1 35.8 %reduce-scatter.42.cloned.1.call-start = ((), (), s32[]{:S(2)}) async-start(), calls=%async_computation.30 | async-start | bytes 7077888 | tf_op jit(solution)/shard_map/reduce_scatter | solution.py:269
  847.2 55.5 %all-gather.38.cloned.1.call-start = ((), (), s32[]{:S(2)}) async-start(), calls=%async_computation.28 | async-start | bytes 3538944 | tf_op jit(solution)/shard_map/all_gather | solution.py:116
  890.4 47.0 %all-gather.36.cloned.1.call-start = ((), (), s32[]{:S(2)}) async-start(), calls=%async_computation.27 | async-start | bytes 3538944 | tf_op jit(solution)/shard_map/all_gather | solution.py:117
  902.6 328.4 %reduce-scatter.44.cloned.1.call-start = ((), (), s32[]{:S(2)}) async-start(), calls=%async_computation.31 | async-start | bytes 7077888 | tf_op jit(solution)/shard_map/reduce_scatter | solution.py:268
  1135.0 98.8 %reduce-scatter.46.cloned.1.call-start = ((), (), s32[]{:S(2)}) async-start(), calls=%async_computation.32 | async-start | bytes 7077888 | tf_op jit(solution)/shard_map/reduce_scatter | solution.py:269
  1153.1 224.4 %all-reduce.16.cloned.1.call-start = ((), (), s32[]{:S(2)}) async-start(), calls=%async_computation.43 | async-start | bytes 221184
  1275.9 249.5 %reduce-scatter.74.cloned.1.call-start = ((), (), s32[]{:S(2)}) async-start(), calls=%async_computation.47 | async-start | bytes 5640192
  1283.2 385.0 %reduce-scatter.72.cloned.1.call-start = ((), (), s32[]{:S(2)}) async-start(), calls=%async_computation.46 | async-start | bytes 5640192
  1291.3 522.5 %reduce-scatter.70.cloned.1.call-start = ((), (), s32[]{:S(2)}) async-start(), calls=%async_computation.45 | async-start | bytes 5640192
  1298.9 701.8 %reduce-scatter.66.cloned.1.call-start = ((), (), s32[]{:S(2)}) async-start(), calls=%async_computation.42 | async-start | bytes 11280384
  1429.3 829.9 %reduce-scatter.68.cloned.1.call-start = ((), (), s32[]{:S(2)}) async-start(), calls=%async_computation.44 | async-start | bytes 16920576
  1456.8 1122.8 %reduce-scatter.54.cloned.1.call-start = ((), (), s32[]{:S(2)}) async-start(), calls=%async_computation.36 | async-start | bytes 22560768 | tf_op jit(solution)/shard_map/reduce_scatter | solution.py:396
  1492.0 1405.8 %reduce-scatter.52.cloned.1.call-start = ((), (), s32[]{:S(2)}) async-start(), calls=%async_computation.35 | async-start | bytes 22560768 | tf_op jit(solution)/shard_map/reduce_scatter | solution.py:390
  1525.3 1384.7 %reduce-scatter.62.cloned.1.call-start = ((), (), s32[]{:S(2)}) async-start(), calls=%async_computation.40 | async-start | bytes 884736
  1527.5 1391.2 %reduce-scatter.60.cloned.1.call-start = ((), (), s32[]{:S(2)}) async-start(), calls=%async_computation.39 | async-start | bytes 884736
  1670.4 1260.4 %reduce-scatter.58.cloned.1.call-start = ((), (), s32[]{:S(2)}) async-start(), calls=%async_computation.38 | async-start | bytes 884736
  1815.9 1126.8 %reduce-scatter.48.cloned.1.call-start = ((), (), s32[]{:S(2)}) async-start(), calls=%async_computation.33 | async-start | bytes 1769472 | tf_op jit(solution)/shard_map/reduce_scatter | solution.py:377
  2003.3 952.3 %reduce-scatter.56.cloned.1.call-start = ((), (), s32[]{:S(2)}) async-start(), calls=%async_computation.37 | async-start | bytes 2654208
  2262.2 635.7 %copy-start.91 = (bf16[1,512,1152]{2,1,0:T(8,128)(2,1)S(1)}, bf16[1,512,1152]{2,1,0:T(8,128)(2,1)}, u32[]{:S(2)}) copy-start(bf16[1,512,1152]{2,1,0:T(8,128)(2,1)} %get-tuple-element.130) | copy-start | bytes 3538948
  2262.2 635.7 %copy-start.92 = (bf16[1,512,1152]{2,1,0:T(8,128)(2,1)S(1)}, bf16[1,512,1152]{2,1,0:T(8,128)(2,1)}, u32[]{:S(2)}) copy-start(bf16[1,512,1152]{2,1,0:T(8,128)(2,1)} %get-tuple-element.133) | copy-start | bytes 3538948
  2262.2 706.1 %reduce-scatter.64.cloned.1.call-start = ((), (), s32[]{:S(2)}) async-start(), calls=%async_computation.41 | async-start | bytes 2654208
  2582.7 398.3 %reduce-scatter.50.cloned.1.call-start = ((), (), s32[]{:S(2)}) async-start(), calls=%async_computation.34 | async-start | bytes 1990656 | tf_op jit(solution)/shard_map/reduce_scatter | solution.py:389
  (212 other events, 4028.2 us)
Sparse Core Ops, SparseCore 0:
  11.6 112.0 all-gather.17
  126.5 83.8 all-gather.25
  212.5 9.4 all-gather.21
  223.4 12.1 all-gather.19
  238.7 65.4 all-gather.23
  307.2 63.1 all-gather.27
  373.7 63.1 all-gather.29
  439.8 132.4 all-gather.31
  575.6 131.6 all-gather.33
  829.2 10.7 reduce-scatter.39
  847.3 11.1 reduce-scatter.41
  890.5 8.1 all-gather.37
  902.7 9.6 all-gather.35
  1135.2 10.1 reduce-scatter.43
  1153.3 10.6 reduce-scatter.45
  1276.0 101.5 all-reduce.15
  1382.7 140.2 reduce-scatter.73
  1528.1 140.1 reduce-scatter.71
  1673.6 140.2 reduce-scatter.69
  1819.5 181.1 reduce-scatter.65
  2007.5 251.6 reduce-scatter.67
  2266.2 313.3 reduce-scatter.53
  2585.6 312.2 reduce-scatter.51
  2900.1 7.0 reduce-scatter.61
  2909.5 9.1 reduce-scatter.59
  2921.5 9.1 reduce-scatter.57
  2932.8 9.7 reduce-scatter.47
  2945.0 10.4 reduce-scatter.55
  2957.8 10.4 reduce-scatter.63
  2971.0 9.9 reduce-scatter.49
where the time goes:
time: 3000 us; the launch traced here: 2990 us
  waiting for transfers between devices  2000 us (67%)
  matrix products  541 us (18%)
  local copies, waits for them, and re-layouts  169 us (6%)
  other arithmetic  140 us (5%)
  blocking collectives  121 us (4%)
    unnamed x41, waiting for transfers between devices  828 us
    reduce_scatter x1, waiting for transfers between devices, body(): lax.psum_scatter(grad_terms[6], 'fsdp', scatter_dimension=0, tiled=True)  317 us
    reduce_scatter x1, waiting for transfers between devices, body(): lax.psum_scatter(grad_terms[5], 'fsdp', scatter_dimension=0, tiled=True)  315 us
    all_gather x1, waiting for transfers between devices, gather_weights(): lax.all_gather(col_parts[5], 'fsdp', axis=0, tiled=True)  127 us
    all_gather x1, waiting for transfers between devices, gather_weights(): lax.all_gather(col_parts[6], 'fsdp', axis=0, tiled=True)  123 us
    unnamed x457, local copies, waits for them, and re-layouts  87.8 us
    all_gather x1, waiting for transfers between devices, gather_weights(): lax.all_gather(col_parts[0], 'fsdp', axis=0, tiled=True)  64 us
    all_gather x1, waiting for transfers between devices, gather_weights(): lax.all_gather(col_parts[2], 'fsdp', axis=0, tiled=True)  61 us
  transfers between devices with their start and end apart: 30, of which 21 were waited for; matrix products, arithmetic and copies ran while one was open for 15% of the time, Pallas kernels for 0%

commit v1 on v0

v1 whole, which is shorter than its diff:
```python
import functools

import jax
import jax.numpy as jnp
from jax import lax
from jax.experimental import pallas as pl
from jax.experimental.pallas import tpu as pltpu
from jax.sharding import PartitionSpec as P

D = 1152
HEADS = 16
HEAD_DIM = 72
MEBI = 1024 * 1024
VMEM_LIMIT = 56 * MEBI
COST_SHARE = 1000

norm_eps = 1e-06
gelu_root = 0.7978845608028654
gelu_cube = 0.044715


def norm_rows(inputs):
    center = inputs - jnp.mean(inputs, axis=-1, keepdims=True)
    spread = jnp.mean(center * center, axis=-1, keepdims=True)
    return center * lax.rsqrt(spread + norm_eps)


def gelu_tanh(inputs):
    return (
        0.5 * inputs * (1.0 + jnp.tanh(gelu_root * (inputs + gelu_cube * inputs * inputs * inputs)))
    )


def modulated(inputs, shift_rows, scale_rows):
    return norm_rows(inputs) * (1.0 + scale_rows) + shift_rows


def flatten(tensor):
    return tensor.reshape(-1, tensor.shape[-1])


def low(values):
    return values.astype(jnp.bfloat16)


def dot_nt(left, right):
    return lax.dot_general(left, right, (((1,), (1,)), ((), ())), preferred_element_type=jnp.float32)


def dot_tn(left, right):
    return lax.dot_general(left, right, (((0,), (0,)), ((), ())), preferred_element_type=jnp.float32)


def cost(flops, bytes_accessed, transcendentals):
    return pl.CostEstimate(
        flops=flops // COST_SHARE,
        bytes_accessed=bytes_accessed // COST_SHARE,
        transcendentals=transcendentals // COST_SHARE,
    )


LANES = 256
LOG2E = 1.4426950408889634
SCALE = HEAD_DIM**-0.5


def contract_last(left, right):
    return lax.dot_general(left, right, (((1,), (1,)), ((), ())), preferred_element_type=jnp.float32)


def matmul(left, right):
    return jnp.dot(left, right, preferred_element_type=jnp.float32)


def head_window(head):
    first = head * HEAD_DIM
    start = pl.multiple_of(jnp.minimum(first // 128 * 128, D - LANES), 128)
    column = start + lax.broadcasted_iota(jnp.int32, (1, LANES), 1)
    inside = (column >= first) & (column < first + HEAD_DIM)
    return pl.ds(start, LANES), inside


def fill_transposed(rows_ref, columns_scr):
    columns_scr[...] = jnp.transpose(rows_ref[0].astype(jnp.float32)).astype(jnp.bfloat16)


def aligned_rows(pair, odd):
    return pl.ds(pl.multiple_of(pair * 144 + 64 * odd, 16), 80)


def head_rows(head):
    return pl.ds(pl.multiple_of(head * HEAD_DIM, 8), HEAD_DIM)


def for_heads(ahead, then):
    ahead(0, 0)

    def two_heads(pair, carry):
        ahead(2 * pair + 1, 1)
        then(2 * pair, pair, 0)
        ahead(jnp.minimum(2 * pair + 2, HEADS - 1), 0)
        then(2 * pair + 1, pair, 1)
        return carry

    lax.fori_loop(0, HEADS // 2, two_heads, 0)


def attend_forward_kernel(q_ref, k_ref, v_ref, o_ref, lse_ref, vt_scr, ot_scr, s_scr):
    @pl.when(pl.program_id(1) == 0)
    def _():
        fill_transposed(v_ref, vt_scr)

    def ahead(head, slot):
        window, inside = head_window(head)
        q_head = q_ref[0, :, window] * inside.astype(jnp.bfloat16)
        s_scr[slot] = contract_last(k_ref[0, :, window], q_head)

    def then(head, pair, slot):
        scores = s_scr[slot]
        top = jnp.max(scores, axis=0, keepdims=True)
        weights = jnp.exp2((scores - top) * (SCALE * LOG2E))
        total = jnp.sum(weights, axis=0, keepdims=True)
        mixed = matmul(vt_scr[aligned_rows(pair, slot), :], weights.astype(jnp.bfloat16))
        ot_scr[head_rows(head), :] = mixed[8 * slot : 8 * slot + HEAD_DIM] * (1.0 / total)
        lse_ref[0, pl.ds(head, 1), :] = top * (SCALE * LOG2E) + jnp.log2(total)

    for_heads(ahead, then)
    o_ref[0] = jnp.transpose(ot_scr[...]).astype(jnp.bfloat16)


def attend_forward(queries, keys, values, row_block):
    (q_arr, q_blk), (k_arr, k_blk), (v_arr, v_blk) = queries, keys, values
    batch, rows, key_rows = q_arr.shape[0], q_arr.shape[1], k_arr.shape[1]
    block = min(row_block, rows)
    return pl.pallas_call(
        attend_forward_kernel,
        grid=(batch, rows // block),
        in_specs=[
            pl.BlockSpec((1, block, D), lambda b, i: (b, i, q_blk)),
            pl.BlockSpec((1, key_rows, D), lambda b, i: (b, 0, k_blk)),
            pl.BlockSpec((1, key_rows, D), lambda b, i: (b, 0, v_blk)),
        ],
        out_specs=[
            pl.BlockSpec((1, block, D), lambda b, i: (b, i, 0)),
            pl.BlockSpec((1, HEADS, block), lambda b, i: (b, 0, i)),
        ],
        out_shape=[
            jax.ShapeDtypeStruct((batch, rows, D), jnp.bfloat16),
            jax.ShapeDtypeStruct((batch, HEADS, rows), jnp.float32),
        ],
        scratch_shapes=[
            pltpu.VMEM((D, key_rows), jnp.bfloat16),
            pltpu.VMEM((D, block), jnp.float32),
            pltpu.VMEM((2, key_rows, block), jnp.float32),
        ],
        compiler_params=pltpu.CompilerParams(vmem_limit_bytes=48 * MEBI),
        cost_estimate=cost(
            flops=4 * batch * rows * key_rows * HEADS * LANES,
            bytes_accessed=4 * batch * (rows + key_rows) * D,
            transcendentals=batch * rows * key_rows * HEADS,
        ),
    )(q_arr, k_arr, v_arr)


def attend_backward_kernel(
    fused, q_ref, k_ref, v_ref, g_ref, o_ref, lse_ref, *rest
):
    if fused:
        out_ref, kt_scr, dk_scr, dv_scr, dqt_scr, dot_scr, s_scr, g_scr = rest
    else:
        dq_ref, dkv_ref, kt_scr, dk_scr, dv_scr, dqt_scr, dot_scr, s_scr, g_scr = rest
    step = pl.program_id(1)
    block = q_ref.shape[1]

    @pl.when(step == 0)
    def _():
        fill_transposed(k_ref, kt_scr)
        dk_scr[...] = jnp.zeros_like(dk_scr)
        dv_scr[...] = jnp.zeros_like(dv_scr)

    products = g_ref[0].astype(jnp.float32) * o_ref[0].astype(jnp.float32)
    head_row = lax.broadcasted_iota(jnp.int32, (HEADS, D), 0) * HEAD_DIM
    column = lax.broadcasted_iota(jnp.int32, (HEADS, D), 1)
    member = ((column >= head_row) & (column < head_row + HEAD_DIM)).astype(jnp.bfloat16)
    high = products.astype(jnp.bfloat16)
    rest_low = (products - high.astype(jnp.float32)).astype(jnp.bfloat16)
    dot_scr[...] = contract_last(member, high) + contract_last(member, rest_low)

    def masked(ref, head):
        window, inside = head_window(head)
        return ref[0, :, window] * inside.astype(jnp.bfloat16)

    def ahead(head, slot):
        window, _ = head_window(head)
        s_scr[slot] = contract_last(k_ref[0, :, window], masked(q_ref, head))
        g_scr[slot] = contract_last(v_ref[0, :, window], masked(g_ref, head))

    def then(head, pair, slot):
        window, _ = head_window(head)
        row = pl.ds(head, 1)
        weights = jnp.exp2(s_scr[slot] * (SCALE * LOG2E) - lse_ref[0, row, :])
        grad_scores = (weights * (g_scr[slot] - dot_scr[row, :])).astype(jnp.bfloat16)
        dv_scr[:, window] += matmul(weights.astype(jnp.bfloat16), masked(g_ref, head))
        dk_scr[:, window] += matmul(grad_scores, masked(q_ref, head))
        dq_rows = matmul(kt_scr[aligned_rows(pair, slot), :], grad_scores)
        dqt_scr[head_rows(head), :] = dq_rows[8 * slot : 8 * slot + HEAD_DIM]

    for_heads(ahead, then)
    grad_q = (jnp.transpose(dqt_scr[...]) * SCALE).astype(jnp.bfloat16)
    if fused:
        out_ref[0, pl.ds(pl.multiple_of(step * block, block), block), :D] = grad_q
    else:
        dq_ref[0] = grad_q

    @pl.when(step == pl.num_programs(1) - 1)
    def _():
        if fused:
            out_ref[0, :, D : 2 * D] = (dk_scr[...] * SCALE).astype(out_ref.dtype)
            out_ref[0, :, 2 * D :] = dv_scr[...].astype(out_ref.dtype)
        else:
            dkv_ref[0, :, :D] = (dk_scr[...] * SCALE).astype(dkv_ref.dtype)
            dkv_ref[0, :, D:] = dv_scr[...].astype(dkv_ref.dtype)


def attend_backward(queries, keys, values, grad_mixed, mixed, lse, row_block, fused, kv_dtype):
    (q_arr, q_blk), (k_arr, k_blk), (v_arr, v_blk) = queries, keys, values
    batch, rows, key_rows = q_arr.shape[0], q_arr.shape[1], k_arr.shape[1]
    block = min(row_block, rows)
    if fused:
        out_specs = [pl.BlockSpec((1, key_rows, 3 * D), lambda b, i: (b, 0, 0))]
        out_shape = [jax.ShapeDtypeStruct((batch, key_rows, 3 * D), jnp.bfloat16)]
    else:
        out_specs = [
            pl.BlockSpec((1, block, D), lambda b, i: (b, i, 0)),
            pl.BlockSpec((1, key_rows, 2 * D), lambda b, i: (b, 0, 0)),
        ]
        out_shape = [
            jax.ShapeDtypeStruct((batch, rows, D), jnp.bfloat16),
            jax.ShapeDtypeStruct((batch, key_rows, 2 * D), kv_dtype),
        ]
    return pl.pallas_call(
        functools.partial(attend_backward_kernel, fused),
        grid=(batch, rows // block),
        in_specs=[
            pl.BlockSpec((1, block, D), lambda b, i: (b, i, q_blk)),
            pl.BlockSpec((1, key_rows, D), lambda b, i: (b, 0, k_blk)),
            pl.BlockSpec((1, key_rows, D), lambda b, i: (b, 0, v_blk)),
            pl.BlockSpec((1, block, D), lambda b, i: (b, i, 0)),
            pl.BlockSpec((1, block, D), lambda b, i: (b, i, 0)),
            pl.BlockSpec((1, HEADS, block), lambda b, i: (b, 0, i)),
        ],
        out_specs=out_specs,
        out_shape=out_shape,
        scratch_shapes=[
            pltpu.VMEM((D, key_rows), jnp.bfloat16),
            pltpu.VMEM((key_rows, D), jnp.float32),
            pltpu.VMEM((key_rows, D), jnp.float32),
            pltpu.VMEM((D, block), jnp.float32),
            pltpu.VMEM((HEADS, block), jnp.float32),
            pltpu.VMEM((2, key_rows, block), jnp.float32),
            pltpu.VMEM((2, key_rows, block), jnp.float32),
        ],
        compiler_params=pltpu.CompilerParams(vmem_limit_bytes=VMEM_LIMIT),
        cost_estimate=cost(
            flops=10 * batch * rows * key_rows * HEADS * LANES,
            bytes_accessed=2 * batch * (3 * rows + 2 * key_rows + 3 * key_rows) * D,
            transcendentals=batch * rows * key_rows * HEADS,
        ),
    )(q_arr, k_arr, v_arr, grad_mixed, mixed, lse)


MLP_TILE = 768


def row_chunks(rows, most=256):
    size = min(most, rows)
    return [slice(first, first + size) for first in range(0, rows, size)]


def lagged(rows, product, use, most=256):
    waiting = None
    for part in row_chunks(rows, most):
        value = product(part)
        if waiting is not None:
            use(*waiting)
        waiting = (part, value)
    use(*waiting)


def mlp_first_kernel(h_ref, w_ref, b_ref, low_ref, slope_ref):
    def product(part):
        return matmul(h_ref[0, part], w_ref[...])

    def use(part, value):
        value = value + b_ref[...]
        square = value * value
        bent = jnp.tanh(value * (gelu_root * gelu_cube * square + gelu_root))
        half = 0.5 * value
        low_ref[0, part] = low(half * bent + half)
        inner = 3.0 * gelu_root * gelu_cube * square + gelu_root
        slope_ref[0, part] = low(half * inner * (1.0 - bent * bent) + (0.5 * bent + 0.5))

    lagged(h_ref.shape[1], product, use)


def mlp_first(h_mlp, whole, bias):
    batch, rows = h_mlp.shape[:2]
    tile = pl.BlockSpec((1, rows, MLP_TILE), lambda b, i: (b, 0, i))
    shape = jax.ShapeDtypeStruct((batch, rows, 2 * D), jnp.bfloat16)
    return pl.pallas_call(
        mlp_first_kernel,
        grid=(batch, 2 * D // MLP_TILE),
        in_specs=[
            pl.BlockSpec((1, rows, D), lambda b, i: (b, 0, 0)),
            pl.BlockSpec((D, MLP_TILE), lambda b, i: (0, i)),
            pl.BlockSpec((1, MLP_TILE), lambda b, i: (0, i)),
        ],
        out_specs=[tile, tile],
        out_shape=[shape, shape],
        compiler_params=pltpu.CompilerParams(vmem_limit_bytes=VMEM_LIMIT),
        cost_estimate=cost(
            flops=4 * batch * rows * D * D,
            bytes_accessed=2 * (batch * rows * 5 * D + 2 * D * D),
            transcendentals=2 * batch * rows * D,
        ),
    )(h_mlp, whole, bias)


def mlp_second_kernel(
    lo_ref, lc_ref, wo_ref, wc_ref, b_ref, x_ref, gate_ref, e_ref,
    out_ref, gm_ref, gate_sum_ref, gm_sum_ref, acc_scr,
):
    step = pl.program_id(1)

    @pl.when(step == 0)
    def _():
        acc_scr[...] = matmul(lo_ref[0], wo_ref[...])

    @pl.when(step == 1)
    def _():
        acc_scr[...] += matmul(lo_ref[0], wo_ref[...])

    @pl.when(step == 2)
    def _():
        acc_scr[...] += matmul(lc_ref[0], wc_ref[...])

    @pl.when(step == 3)
    def _():
        gate = gate_ref[0]
        sums = [0.0, 0.0]

        def product(part):
            return acc_scr[part] + matmul(lc_ref[0, part], wc_ref[...])

        def use(part, value):
            mlp_out = value + b_ref[...]
            grad = e_ref[0, part].astype(jnp.float32)
            out_ref[0, part] = low(x_ref[0, part] + gate * mlp_out)
            grad_mlp = low(gate * grad)
            gm_ref[0, part] = grad_mlp
            sums[0] += jnp.sum(grad * mlp_out, axis=0, keepdims=True)
            sums[1] += jnp.sum(grad_mlp.astype(jnp.float32), axis=0, keepdims=True)

        lagged(lo_ref.shape[1], product, use)
        gate_sum_ref[0], gm_sum_ref[0] = sums


def mlp_second(lows, wholes, bias, after_cross, gate, cotangent):
    batch, rows = after_cross.shape[:2]
    full = pl.BlockSpec((1, rows, D), lambda b, k: (b, 0, 0))
    row = pl.BlockSpec((1, 1, D), lambda b, k: (b, 0, 0))

    def first(k):
        return jnp.minimum(k, 1)

    def later(k):
        return jnp.maximum(k - 2, 0)

    return pl.pallas_call(
        mlp_second_kernel,
        grid=(batch, 4),
        in_specs=[
            pl.BlockSpec((1, rows, D), lambda b, k: (b, 0, first(k))),
            pl.BlockSpec((1, rows, D), lambda b, k: (b, 0, later(k))),
            pl.BlockSpec((D, D), lambda b, k: (0, 2 + first(k))),
            pl.BlockSpec((D, D), lambda b, k: (0, 2 + later(k))),
            pl.BlockSpec((1, D), lambda b, k: (0, 0)),
            full,
            row,
            full,
        ],
        out_specs=[full, full, row, row],
        out_shape=[
            jax.ShapeDtypeStruct((batch, rows, D), jnp.bfloat16),
            jax.ShapeDtypeStruct((batch, rows, D), jnp.bfloat16),
            jax.ShapeDtypeStruct((batch, 1, D), jnp.float32),
            jax.ShapeDtypeStruct((batch, 1, D), jnp.float32),
        ],
        scratch_shapes=[pltpu.VMEM((rows, D), jnp.float32)],
        compiler_params=pltpu.CompilerParams(vmem_limit_bytes=56 * MEBI),
        cost_estimate=cost(
            flops=8 * batch * rows * D * D,
            bytes_accessed=batch * rows * D * 18 + 8 * D * D,
            transcendentals=0,
        ),
    )(*lows, *wholes, bias, after_cross, gate, cotangent)


def mlp_slope_kernel(g_ref, w_ref, slope_ref, gp_ref, sum_ref):
    sums = [0.0]

    def product(part):
        return contract_last(g_ref[0, part], w_ref[...])

    def use(part, value):
        grad = low(value * slope_ref[0, part].astype(jnp.float32))
        gp_ref[0, part] = grad
        sums[0] += jnp.sum(grad.astype(jnp.float32), axis=0, keepdims=True)

    lagged(g_ref.shape[1], product, use)
    sum_ref[0] = sums[0]


def mlp_slope(grad_mlp, whole, slope):
    batch, rows = grad_mlp.shape[:2]
    return pl.pallas_call(
        mlp_slope_kernel,
        grid=(batch, 2),
        in_specs=[
            pl.BlockSpec((1, rows, D), lambda b, i: (b, 0, 0)),
            pl.BlockSpec((D, D), lambda b, i: (0, 2 + i)),
            pl.BlockSpec((1, rows, D), lambda b, i: (b, 0, i)),
        ],
        out_specs=[
            pl.BlockSpec((1, rows, D), lambda b, i: (b, 0, i)),
            pl.BlockSpec((1, 1, D), lambda b, i: (b, 0, i)),
        ],
        out_shape=[
            jax.ShapeDtypeStruct((batch, rows, 2 * D), jnp.bfloat16),
            jax.ShapeDtypeStruct((batch, 1, 2 * D), jnp.float32),
        ],
        compiler_params=pltpu.CompilerParams(vmem_limit_bytes=42 * MEBI),
        cost_estimate=cost(
            flops=4 * batch * rows * D * D,
            bytes_accessed=2 * (batch * rows * 5 * D + 2 * D * D),
            transcendentals=0,
        ),
    )(grad_mlp, whole, slope)


def norm_backward(inputs, grad, scale_rows):
    center = inputs - jnp.mean(inputs, axis=-1, keepdims=True)
    spread = jnp.mean(center * center, axis=-1, keepdims=True)
    root = lax.rsqrt(spread + norm_eps)
    normed = center * root
    grad_shift = jnp.sum(grad, axis=0, keepdims=True)
    grad_scale = jnp.sum(grad * normed, axis=0, keepdims=True)
    inner = grad * (1.0 + scale_rows)
    along = jnp.mean(inner * normed, axis=-1, keepdims=True)
    inner = root * (inner - jnp.mean(inner, axis=-1, keepdims=True) - normed * along)
    return inner, grad_shift, grad_scale


def mlp_input_kernel(
    go_ref, gc_ref, wo_ref, wc_ref, x_ref, scale_ref, e_ref,
    gx_ref, gl_ref, shift_sum_ref, scale_sum_ref, gl_sum_ref, acc_scr,
):
    step = pl.program_id(1)

    @pl.when(step == 0)
    def _():
        acc_scr[...] = jnp.zeros_like(acc_scr)

    @pl.when(step < 3)
    def _():
        acc_scr[...] += contract_last(go_ref[0], wo_ref[...])

    @pl.when((step >= 3) & (step < 5))
    def _():
        acc_scr[...] += contract_last(gc_ref[0], wc_ref[...])

    @pl.when(step == 5)
    def _():
        sums = [0.0, 0.0, 0.0]

        def product(part):
            return acc_scr[part] + contract_last(gc_ref[0, part], wc_ref[...])

        def use(part, grad):
            inner, grad_shift, grad_scale = norm_backward(x_ref[0, part], grad, scale_ref[0])
            inner += e_ref[0, part].astype(jnp.float32)
            gx_ref[0, part] = inner
            gl_ref[0, part] = low(inner)
            low_sum = jnp.sum(low(inner).astype(jnp.float32), axis=0, keepdims=True)
            for at, new in enumerate((grad_shift, grad_scale, low_sum)):
                sums[at] += new

        lagged(go_ref.shape[1], product, use)
        shift_sum_ref[0], scale_sum_ref[0], gl_sum_ref[0] = sums


def mlp_input(grads, wholes, after_cross, scale_rows, cotangent):
    batch, rows = after_cross.shape[:2]
    full = pl.BlockSpec((1, rows, D), lambda b, k: (b, 0, 0))
    row = pl.BlockSpec((1, 1, D), lambda b, k: (b, 0, 0))
    row_shape = jax.ShapeDtypeStruct((batch, 1, D), jnp.float32)

    def first(k):
        return jnp.minimum(k, 2)

    def later(k):
        return jnp.maximum(k - 3, 0)

    return pl.pallas_call(
        mlp_input_kernel,
        grid=(batch, 6),
        in_specs=[
            pl.BlockSpec((1, rows, MLP_TILE), lambda b, k: (b, 0, first(k))),
            pl.BlockSpec((1, rows, MLP_TILE), lambda b, k: (b, 0, later(k))),
            pl.BlockSpec((D, MLP_TILE), lambda b, k: (0, first(k))),
            pl.BlockSpec((D, MLP_TILE), lambda b, k: (0, later(k))),
            full,
            row,
            full,
        ],
        out_specs=[full, full, row, row, row],
        out_shape=[
            jax.ShapeDtypeStruct((batch, rows, D), jnp.float32),
            jax.ShapeDtypeStruct((batch, rows, D), jnp.bfloat16),
            row_shape,
            row_shape,
            row_shape,
        ],
        scratch_shapes=[pltpu.VMEM((rows, D), jnp.float32)],
        compiler_params=pltpu.CompilerParams(vmem_limit_bytes=56 * MEBI),
        cost_estimate=cost(
            flops=8 * batch * rows * D * D,
            bytes_accessed=batch * rows * D * 20 + 8 * D * D,
            transcendentals=0,
        ),
    )(*grads, *wholes, after_cross, scale_rows, cotangent)


def attend_input_kernel(
    g_ref, w_ref, x_ref, scale_ref, r_ref,
    gx_ref, shift_sum_ref, scale_sum_ref, g_sum_ref, acc_scr,
):
    step = pl.program_id(1)
    g_sum_ref[0] = jnp.sum(g_ref[0].astype(jnp.float32), axis=0, keepdims=True)

    @pl.when(step == 0)
    def _():
        acc_scr[...] = contract_last(g_ref[0], w_ref[...])

    @pl.when(step == 1)
    def _():
        acc_scr[...] += contract_last(g_ref[0], w_ref[...])

    @pl.when(step == 2)
    def _():
        sums = [0.0, 0.0]

        def product(part):
            return acc_scr[part] + contract_last(g_ref[0, part], w_ref[...])

        def use(part, grad):
            inputs = x_ref[0, part].astype(jnp.float32)
            inner, grad_shift, grad_scale = norm_backward(inputs, grad, scale_ref[0])
            gx_ref[0, part] = inner + r_ref[0, part]
            sums[0] += grad_shift
            sums[1] += grad_scale

        lagged(g_ref.shape[1], product, use)
        shift_sum_ref[0], scale_sum_ref[0] = sums


def attend_input(grad_qkv, weight, tokens, scale_rows, grad_attn):
    batch, rows = tokens.shape[:2]
    full = pl.BlockSpec((1, rows, D), lambda b, k: (b, 0, 0))
    row = pl.BlockSpec((1, 1, D), lambda b, k: (b, 0, 0))
    row_shape = jax.ShapeDtypeStruct((batch, 1, D), jnp.float32)
    return pl.pallas_call(
        attend_input_kernel,
        grid=(batch, 3),
        in_specs=[
            pl.BlockSpec((1, rows, D), lambda b, k: (b, 0, k)),
            pl.BlockSpec((D, D), lambda b, k: (0, k)),
            full,
            row,
            full,
        ],
        out_specs=[full, row, row, pl.BlockSpec((1, 1, D), lambda b, k: (b, 0, k))],
        out_shape=[
            jax.ShapeDtypeStruct((batch, rows, D), jnp.float32),
            row_shape,
            row_shape,
            jax.ShapeDtypeStruct((batch, 1, 3 * D), jnp.float32),
        ],
        scratch_shapes=[pltpu.VMEM((rows, D), jnp.float32)],
        compiler_params=pltpu.CompilerParams(vmem_limit_bytes=56 * MEBI),
        cost_estimate=cost(
            flops=6 * batch * rows * D * D,
            bytes_accessed=batch * rows * D * 16 + 6 * D * D,
            transcendentals=0,
        ),
    )(grad_qkv, weight, tokens, scale_rows, grad_attn)


def self_output_kernel(
    m_ref, wo_ref, bo_ref, x_ref, gate_ref, wq_ref, bq_ref, proj_ref, sum_ref, low_ref, query_ref
):
    def product(part):
        proj = matmul(m_ref[0, part], wo_ref[...]) + bo_ref[...]
        proj_ref[0, part] = proj
        after_attn = x_ref[0, part].astype(jnp.float32) + gate_ref[0] * proj
        sum_ref[0, part] = after_attn
        low_ref[0, part] = low(after_attn)
        return low(after_attn)

    def use(part, value):
        query_ref[0, part] = low(matmul(value, wq_ref[...]) + bq_ref[...])

    lagged(m_ref.shape[1], product, use, 128)


def self_output(mixed, w_out, out_bias, tokens, gate, w_query, query_bias):
    batch, rows = mixed.shape[:2]
    block = min(256, rows)
    part = pl.BlockSpec((1, block, D), lambda b, i: (b, i, 0))
    whole = pl.BlockSpec((D, D), lambda b, i: (0, 0))
    row = pl.BlockSpec((1, D), lambda b, i: (0, 0))
    wide = jax.ShapeDtypeStruct((batch, rows, D), jnp.float32)
    narrow = jax.ShapeDtypeStruct((batch, rows, D), jnp.bfloat16)
    return pl.pallas_call(
        self_output_kernel,
        grid=(batch, rows // block),
        in_specs=[
            part,
            whole,
            row,
            part,
            pl.BlockSpec((1, 1, D), lambda b, i: (b, 0, 0)),
            whole,
            row,
        ],
        out_specs=[part] * 4,
        out_shape=[wide, wide, narrow, narrow],
        compiler_params=pltpu.CompilerParams(vmem_limit_bytes=44 * MEBI),
        cost_estimate=cost(
            flops=4 * batch * rows * D * D,
            bytes_accessed=batch * rows * D * 16 + 4 * D * D,
            transcendentals=0,
        ),
    )(mixed, w_out, out_bias, tokens, gate, w_query, query_bias)


def cross_output_kernel(m_ref, w_ref, b_ref, x_ref, shift_ref, scale_ref, sum_ref, h_ref):
    def product(part):
        return matmul(m_ref[0, part], w_ref[...])

    def use(part, value):
        after_cross = x_ref[0, part] + (value + b_ref[...])
        sum_ref[0, part] = after_cross
        h_ref[0, part] = low(modulated(after_cross, shift_ref[0], scale_ref[0]))

    lagged(m_ref.shape[1], product, use, 128)


def cross_output(mixed, weight, bias, after_attn, shift_rows, scale_rows):
    batch, rows = mixed.shape[:2]
    block = min(256, rows)
    part = pl.BlockSpec((1, block, D), lambda b, i: (b, i, 0))
    row = pl.BlockSpec((1, 1, D), lambda b, i: (b, 0, 0))
    return pl.pallas_call(
        cross_output_kernel,
        grid=(batch, rows // block),
        in_specs=[
            part,
            pl.BlockSpec((D, D), lambda b, i: (0, 0)),
            pl.BlockSpec((1, D), lambda b, i: (0, 0)),
            part,
            row,
            row,
        ],
        out_specs=[part, part],
        out_shape=[
            jax.ShapeDtypeStruct((batch, rows, D), jnp.float32),
            jax.ShapeDtypeStruct((batch, rows, D), jnp.bfloat16),
        ],
        compiler_params=pltpu.CompilerParams(vmem_limit_bytes=36 * MEBI),
        cost_estimate=cost(
            flops=2 * batch * rows * D * D,
            bytes_accessed=batch * rows * D * 12 + 2 * D * D,
            transcendentals=0,
        ),
    )(mixed, weight, bias, after_attn, shift_rows, scale_rows)


def chip_flip(count, bit):
    return [(chip, chip ^ bit) for chip in range(count)]


def chip_shift(count, steps):
    return [(chip, (chip + 4 * steps) % count) for chip in range(count)]


def pick(tensor, index, axis):
    return lax.dynamic_index_in_dim(tensor, index, axis, keepdims=False)


def stack_kernel(*refs):
    for at, ref in enumerate(refs[:-1]):
        refs[-1][at] = ref[...]


def column_pieces(shard):
    count = lax.axis_size("fsdp")
    blocks = [shard] + [
        lax.ppermute(shard, "fsdp", chip_shift(count, -step)) for step in range(1, count // 4)
    ]
    return pl.pallas_call(
        stack_kernel,
        out_shape=jax.ShapeDtypeStruct((len(blocks), *shard.shape), shard.dtype),
        compiler_params=pltpu.CompilerParams(vmem_limit_bytes=32 * MEBI),
    )(*blocks)


def near_pieces(column):
    count = lax.axis_size("fsdp")
    return [
        column,
        lax.ppermute(column, "fsdp", chip_flip(count, 2)),
        lax.ppermute(column, "fsdp", chip_flip(count, 1)),
    ]


def far_pieces(near, split):
    count = lax.axis_size("fsdp")
    return [
        lax.ppermute(near[1][..., :split], "fsdp", chip_flip(count, 1)),
        lax.ppermute(near[2][..., split:], "fsdp", chip_flip(count, 2)),
    ]


def piece_columns(refs, start, width):
    blocks = []
    for ref in refs:
        columns = ref.shape[2]
        first, last = max(start, 0), min(start + width, columns)
        if first < last:
            blocks.append(ref[0, :, first:last])
        start -= columns
    return blocks


def assemble_kernel(regions, counts, place, *refs):
    y, x, core = place[1], place[2], place[3]
    sides = []
    for count in counts:
        sides.append(refs[:count])
        refs = refs[count:]

    def write(order):
        for flip_y, flip_x in ((0, 0), (1, 0), (0, 1), (1, 1)):
            chip = (y ^ flip_y) * 2 + (x ^ flip_x)
            near = flip_y + 2 * flip_x
            for out, (start, width) in zip(refs, regions):
                blocks = []
                for side in order:
                    pieces = sides[side][near : near + 1] if near < 3 else sides[side][3:]
                    blocks.extend(piece_columns(pieces, start, width))
                out[0, chip] = blocks[0] if len(blocks) == 1 else jnp.concatenate(blocks, axis=1)

    if len(counts) == 1:
        write((0,))
    else:
        pl.when(core == 0)(lambda: write((0, 1)))
        pl.when(core != 0)(lambda: write((1, 0)))


def assemble(sides, regions):
    count = lax.axis_size("fsdp")
    deep = count // 4
    chip = lax.axis_index("fsdp")
    place = jnp.stack([chip // 4, chip // 2 % 2, chip % 2, lax.axis_index("seq")])
    rows = sides[0][0].shape[1]
    widths = [len(sides) * width for _, width in regions]

    def from_z(i, place):
        return (lax.rem(i - place[0] + deep, deep), 0, 0)

    ins = [piece for side in sides for piece in side]
    outs = pl.pallas_call(
        functools.partial(assemble_kernel, regions, [len(side) for side in sides]),
        grid_spec=pltpu.PrefetchScalarGridSpec(
            num_scalar_prefetch=1,
            grid=(deep,),
            in_specs=[pl.BlockSpec((1, *piece.shape[1:]), from_z) for piece in ins],
            out_specs=[
                pl.BlockSpec((1, 4, rows, width), lambda i, place: (i, 0, 0, 0))
                for width in widths
            ],
        ),
        out_shape=[
            jax.ShapeDtypeStruct((deep, 4, rows, width), jnp.bfloat16) for width in widths
        ],
        compiler_params=pltpu.CompilerParams(vmem_limit_bytes=48 * MEBI),
        cost_estimate=cost(
            flops=0, bytes_accessed=16 * deep * rows * sum(widths), transcendentals=0
        ),
    )(place.astype(jnp.int32), *ins)
    return [out.reshape(count * rows, out.shape[-1]) for out in outs]


def gather_small(shard):
    count = lax.axis_size("fsdp")
    deep = count // 4
    z, y, x = chip_place()
    both = jnp.stack([shard, lax.ppermute(shard, "fsdp", chip_flip(count, 2))])
    both = jnp.where(y == 0, both, both[::-1])
    four = jnp.stack([both, lax.ppermute(both, "fsdp", chip_flip(count, 1))], axis=1)
    four = jnp.where(x == 0, four, four[:, ::-1])
    blocks = [four] + [
        lax.ppermute(four, "fsdp", chip_shift(count, -step)) for step in range(1, deep)
    ]
    blocks = jnp.stack(blocks + blocks[:-1])
    blocks = lax.dynamic_slice_in_dim(blocks, lax.rem(deep - z, deep), deep, 0)
    return blocks.reshape(count * shard.shape[0], shard.shape[1])


def chip_place():
    chip = lax.axis_index("fsdp")
    return chip // 4, chip // 2 % 2, chip % 2


def picks(blocks, index, axis):
    return jnp.concatenate([pick(block, index, axis) for block in blocks], axis=-1)


def sum_first(terms, x_first):
    count = lax.axis_size("fsdp")
    _, y, x = chip_place()
    blocks = [
        term.reshape(count // 4, 2, 2, term.shape[0] // count, term.shape[1]) for term in terms
    ]
    return blocks, picks(blocks, 1 - x, 2) if x_first else picks(blocks, 1 - y, 1)


def across_chips(kept, gone, bit, earlier):
    came = lax.ppermute(gone, "fsdp", chip_flip(lax.axis_size("fsdp"), bit))
    return low(kept.astype(jnp.float32) + after(came, earlier).astype(jnp.float32))


def sum_second(blocks, gone, x_first, earlier):
    _, y, x = chip_place()
    kept = picks(blocks, x, 2) if x_first else picks(blocks, y, 1)
    sums = across_chips(kept, gone, 1 if x_first else 2, earlier)
    return sums, pick(sums, 1 - y if x_first else 1 - x, 1)


def sum_third(sums, gone, x_first, earlier):
    _, y, x = chip_place()
    return across_chips(pick(sums, y if x_first else x, 1), gone, 2 if x_first else 1, earlier)


def along_z(*columns):
    column = jnp.concatenate(columns, axis=-1)
    deep, z = column.shape[0], chip_place()[0]
    return column, [pick(column, lax.rem(z + step, deep), 0) for step in range(1, deep)]


def sum_last(column, gones, earlier):
    count = lax.axis_size("fsdp")
    total = pick(column, chip_place()[0], 0).astype(jnp.float32)
    for step, gone in enumerate(gones, 1):
        came = lax.ppermute(gone, "fsdp", chip_shift(count, step))
        total += after(came, earlier).astype(jnp.float32)
    return total


def tie(*values):
    return lax.optimization_barrier(values)


def after(value, earlier):
    return lax.optimization_barrier((value, earlier))[0]


def column_sum(rows):
    return jnp.sum(rows.astype(jnp.float32), axis=0, keepdims=True)


def body(
    tokens, timestep, text, cotangent, vectors, w_qkv, w_out, w_query2, w_kv2, w_out2, w_fc1, w_fc2
):
    cores = lax.axis_size("seq")
    images = tokens.shape[0]
    swap = cores == 2 and images == 2
    core = lax.axis_index("seq")
    other = 1 - core
    across = [(0, 1), (1, 0)]
    rows_here = w_fc1.shape[0]

    def trade(rows):
        mine = lax.dynamic_slice_in_dim(rows, core, 1, 0)
        gone = lax.dynamic_slice_in_dim(rows, other, 1, 0)
        return jnp.concatenate([mine, lax.ppermute(gone, "seq", across)], axis=1)

    def trade_back(rows):
        half = rows.shape[1] // 2
        return by_core(rows[:, :half], pair(rows[:, half:]), 0)

    def by_core(mine, came, axis):
        return jnp.where(
            core == 0,
            jnp.concatenate([mine, came], axis=axis),
            jnp.concatenate([came, mine], axis=axis),
        )

    def pair(part):
        return lax.ppermute(part, "seq", across)

    def mlp_shard():
        here = w_fc1.reshape(rows_here, -1, 2, 2, rows_here)
        gone, mine = pick(here, other, 2), pick(here, core, 2)
        first = by_core(mine, pair(gone), 1)
        first = first.transpose(0, 2, 1, 3).reshape(rows_here, -1)
        here = w_fc2.reshape(2, 2, rows_here, -1)
        gone, mine = pick(here, other, 0), pick(here, core, 0)
        second = by_core(mine, pair(gone), 2)
        return jnp.concatenate([first, second[0], second[1]], axis=1)

    def whole_rest(near, earlier):
        near = after(near, earlier)
        pieces = [*near, *far_pieces(near, 1408)]
        half = w_out.shape[1]
        return assemble(
            [pieces, [pair(piece) for piece in pieces]],
            [(0, half), (half, half), (2 * half, 2 * half), (4 * half, half)],
        )

    def gather_plain():
        whole = [
            lax.all_gather(
                lax.all_gather(part, "fsdp", axis=0, tiled=True), "seq", axis=1, tiled=True
            )
            for part in (w_qkv, w_out, w_query2, w_kv2, w_out2, w_fc1, w_fc2)
        ]
        first, second = whole[5:]
        mlp = [
            jnp.concatenate(
                [
                    first[:, 2 * part * D : 2 * (part + 1) * D],
                    second[2 * part * D : (2 * part + 1) * D],
                    second[(2 * part + 1) * D : 2 * (part + 1) * D],
                ],
                axis=1,
            )
            for part in range(2)
        ]
        return (*whole[:5], mlp)

    def core_parts(right):
        width = (right.shape[1] // 2 + 127) // 128 * 128
        low_part, high_part = right[:, :width], right[:, -width:]
        return (
            jnp.where(core == 0, high_part, low_part),
            jnp.where(core == 0, low_part, high_part),
        )

    def pair_send(left, right):
        return low(dot_tn(left, core_parts(right)[0]))

    def pair_sum(left, right, sent):
        return low(dot_tn(left, core_parts(right)[1]) + pair(sent).astype(jnp.float32))

    def pair_grad(left, right):
        return pair_sum(left, right, pair_send(left, right))

    def own_half(wide, place):
        return jnp.where(place == 0, wide[:, :-64], wide[:, 64:])

    def weight_grad(left, right):
        return scatter_plain(low(dot_tn(left, right)))

    def scatter_plain(full):
        part = lax.psum_scatter(full, "seq", scatter_dimension=1, tiled=True)
        return lax.psum_scatter(part, "fsdp", scatter_dimension=0, tiled=True).astype(jnp.float32)

    if swap:
        shard, vectors, tokens, text, cotangent = tie(
            mlp_shard(), vectors, tokens, text, cotangent
        )
        mlp_own = lax.all_gather(shard, "fsdp", axis=0, tiled=True)
        column = column_pieces(w_qkv)
        vec = gather_small(jnp.pad(vectors, ((0, 0), (0, 128 - vectors.shape[1]))))
        tokens, text, cotangent = trade(tokens), trade(text), trade(cotangent)
        column, vec, tokens, text, cotangent, others = tie(
            column, vec, tokens, text, cotangent, (w_out, w_query2, w_kv2, w_out2)
        )
        near = near_pieces(column)
        rest = column_pieces(jnp.concatenate(others, axis=1))
        far, rest = tie(far_pieces(near, 896), rest)
        rest_near = near_pieces(rest)
        pieces = [*near, *far]
        (wf_qkv,) = assemble([pieces, [pair(piece) for piece in pieces]], [(0, w_qkv.shape[1])])
        vec = vec.T[: vectors.shape[1]].astype(jnp.float32)
        timestep = lax.dynamic_slice_in_dim(timestep, core, 1, 0)
    batch, rows = tokens.shape[0], tokens.shape[1]
    if not swap:
        vec = lax.all_gather(vectors, "fsdp", axis=0, tiled=True).T.astype(jnp.float32)
        wf_qkv, wf_out, wf_query2, wf_kv2, wf_out2, mlp = gather_plain()

    def unflat(tensor):
        return tensor.reshape(batch, rows, tensor.shape[-1])

    inputs = tokens.astype(jnp.float32)
    modulation = vec[None, :6] + timestep.astype(jnp.float32).reshape(batch, 6, D)
    zero_bias = jnp.zeros((1, D), jnp.float32)
    h_attn = lax.optimization_barrier(
        low(modulated(inputs, modulation[:, 0:1], modulation[:, 1:2]))
    )
    qkv_bias = jnp.concatenate([vec[6:7], zero_bias, vec[7:8]], axis=1)
    qkv_rows = unflat(low(matmul(flatten(h_attn), wf_qkv) + qkv_bias))
    if swap:
        self_qkv = ((qkv_rows, 0), (qkv_rows, 1), (qkv_rows, 2))
    else:
        all_kv = lax.all_gather(qkv_rows[..., D:], "seq", axis=1, tiled=True)
        self_qkv = ((qkv_rows, 0), (all_kv, 0), (all_kv, 1))
    attn_low, self_lse = attend_forward(*self_qkv, 512)
    if swap:
        wf_out, wf_query2, wf_kv2, wf_out2 = whole_rest(rest_near, attn_low)
    attn_proj, after_attn, after_low, cross_query = self_output(
        attn_low, wf_out, vec[8:9], tokens, modulation[:, 2:3], wf_query2, vec[9:10]
    )
    kv_bias = jnp.concatenate([zero_bias, vec[10:11]], axis=1)
    text_kv = low(matmul(flatten(text), wf_kv2) + kv_bias).reshape(batch, text.shape[1], 2 * D)
    if not swap:
        text_kv = lax.all_gather(text_kv, "seq", axis=1, tiled=True)
    cross_qkv = ((cross_query, 0), (text_kv, 0), (text_kv, 1))
    cross_low, cross_lse = attend_forward(*cross_qkv, 1024)
    after_cross, h_mlp = cross_output(
        cross_low, wf_out2, vec[11:12], after_attn, modulation[:, 3:4], modulation[:, 4:5]
    )
    fc1_bias = vec[13:].reshape(1, -1)
    if swap:
        fc1_bias = fc1_bias.reshape(-1, 2, 2, rows_here)
        biases = [
            pick(fc1_bias, place, 1).transpose(1, 0, 2).reshape(1, -1) for place in (core, other)
        ]
    else:
        biases = [fc1_bias[:, : 2 * D], fc1_bias[:, 2 * D :]]
    if swap:
        mlp = (mlp_own, pair(after(mlp_own, h_mlp)))
    hidden = [mlp_first(h_mlp, whole, bias) for whole, bias in zip(mlp, biases)]
    lows = [hidden_low for hidden_low, _ in hidden]
    result, grad_mlp, grad_gate_mlp, fc2_sums = mlp_second(
        lows, mlp, vec[12:13], after_cross, modulation[:, 5:6], cotangent
    )

    flat_h, flat_gm = flatten(h_mlp), flatten(grad_mlp)
    if swap:
        own_low, other_low = flatten(lows[0]), flatten(lows[1])
        sent = low(dot_tn(other_low, flat_gm))
        sent, grad_mlp = tie(sent, grad_mlp)
        other_pre, other_sums = mlp_slope(grad_mlp, mlp[1], hidden[1][1])
        fc2_part = low(dot_tn(own_low, flat_gm) + pair(sent).astype(jnp.float32))
        fc2_x, fc2_gone_x = sum_first([fc2_part[:D]], True)
        fc2_y, fc2_gone_y = sum_first([fc2_part[D:]], False)
        fc2_gone_x, fc2_gone_y, other_pre, grad_mlp = tie(
            fc2_gone_x, fc2_gone_y, other_pre, grad_mlp
        )
        sent = low(dot_tn(flat_h, flatten(other_pre)))
        sent, grad_mlp = tie(sent, grad_mlp)
        own_pre, own_sums = mlp_slope(grad_mlp, mlp[0], hidden[0][1])
        fc2_x, fc2_gone_x = sum_second(fc2_x, fc2_gone_x, True, own_pre)
        fc2_y, fc2_gone_y = sum_second(fc2_y, fc2_gone_y, False, own_pre)
        fc2_gone_x, fc2_gone_y, own_pre = tie(fc2_gone_x, fc2_gone_y, own_pre)
        fc1_part = low(dot_tn(flat_h, flatten(own_pre)) + pair(sent).astype(jnp.float32))
        fc1_x, fc1_gone_x = sum_first([fc1_part[:, :D]], True)
        fc1_y, fc1_gone_y = sum_first([fc1_part[:, D:]], False)
        own_pre, fc1_gone_x, fc1_gone_y = tie(own_pre, fc1_gone_x, fc1_gone_y)
        result = after(result, fc1_gone_x)
        grads_pre, fc1_sums = [own_pre, other_pre], [own_sums, other_sums]
    else:
        slopes = [mlp_slope(grad_mlp, whole, slope) for whole, (_, slope) in zip(mlp, hidden)]
        grads_pre = [grad_pre for grad_pre, _ in slopes]
        fc1_sums = [sums for _, sums in slopes]
    fc1_sums = [jnp.sum(sums, axis=0) for sums in fc1_sums]
    grad_cross, grad_proj2, grad_shift_mlp, grad_scale_mlp, out2_sums = mlp_input(
        grads_pre, mlp, after_cross, modulation[:, 4:5], cotangent
    )
    grad_proj2 = flatten(grad_proj2)
    if swap:
        fc1_x, fc1_gone_x = sum_second(fc1_x, fc1_gone_x, True, grad_proj2)
        fc1_y, fc1_gone_y = sum_second(fc1_y, fc1_gone_y, False, grad_proj2)
        fc1_gone_x, fc1_gone_y, grad_proj2 = tie(fc1_gone_x, fc1_gone_y, grad_proj2)
    grad_mixed2 = unflat(low(dot_nt(grad_proj2, wf_out2)))
    if swap:
        out2_part = pair_grad(flatten(cross_low), grad_proj2)
        grad_mixed2, out2_part = tie(grad_mixed2, out2_part)
    grad_q2, grad_kv = attend_backward(
        *cross_qkv, grad_mixed2, cross_low, cross_lse, 1024, False,
        jnp.bfloat16 if swap else jnp.float32,
    )
    if not swap:
        grad_kv = low(lax.psum_scatter(grad_kv, "seq", scatter_dimension=1, tiled=True))
    grad_kv, grad_q2 = flatten(grad_kv), flatten(grad_q2)
    if swap:
        mlp_column, mlp_gones = along_z(
            sum_third(fc1_x, fc1_gone_x, True, grad_q2),
            sum_third(fc1_y, fc1_gone_y, False, grad_q2),
            sum_third(fc2_x, fc2_gone_x, True, grad_q2),
            sum_third(fc2_y, fc2_gone_y, False, grad_q2),
        )
        mlp_gones, grad_q2, grad_kv = tie(mlp_gones, grad_q2, grad_kv)
    grad_text = dot_nt(grad_kv, wf_kv2).reshape(text.shape)
    grad_attn = grad_cross + unflat(dot_nt(grad_q2, wf_query2))
    grad_gate_attn = jnp.sum(grad_attn * attn_proj, axis=1, keepdims=True)
    grad_proj1 = flatten(low(modulation[:, 2:3] * grad_attn))
    grad_mixed1 = unflat(low(dot_nt(grad_proj1, wf_out)))
    if swap:
        rest_x, gone_x = sum_first(
            [
                pair_grad(flatten(text), grad_kv),
                pair_grad(flatten(attn_low), grad_proj1),
            ],
            True,
        )
        rest_y, gone_y = sum_first(
            [out2_part, pair_grad(flatten(after_low), grad_q2)], False
        )
        gone_x, gone_y, grad_mixed1 = tie(gone_x, gone_y, grad_mixed1)
        (grad_qkv_low,) = attend_backward(
            *self_qkv, grad_mixed1, attn_low, self_lse, 256, True, jnp.bfloat16
        )
        grad_qkv_low = flatten(grad_qkv_low)
        rest_x, gone_x = sum_second(rest_x, gone_x, True, grad_qkv_low)
        rest_y, gone_y = sum_second(rest_y, gone_y, False, grad_qkv_low)
        mlp_part = sum_last(mlp_column, mlp_gones, grad_qkv_low)
        gone_x, gone_y, mlp_part, grad_qkv_low = tie(gone_x, gone_y, mlp_part, grad_qkv_low)
        qkv_part = pair_grad(flatten(h_attn), grad_qkv_low)
        columns = qkv_part.shape[1] // 2
        qkv_x, qkv_gone_x = sum_first([qkv_part[:, :columns]], True)
        qkv_y, qkv_gone_y = sum_first([qkv_part[:, columns:]], False)
        column, gones = along_z(
            sum_third(rest_x, gone_x, True, qkv_gone_x),
            sum_third(rest_y, gone_y, False, qkv_gone_y),
        )
        gones, qkv_gone_x, qkv_gone_y, grad_qkv_low = tie(
            gones, qkv_gone_x, qkv_gone_y, grad_qkv_low
        )
        grad_tokens, grad_shift_attn, grad_scale_attn, qkv_sums = attend_input(
            unflat(grad_qkv_low), wf_qkv, tokens, modulation[:, 1:2], grad_attn
        )
        qkv_x, gone_x = sum_second(qkv_x, qkv_gone_x, True, grad_shift_attn)
        qkv_y, gone_y = sum_second(qkv_y, qkv_gone_y, False, grad_shift_attn)
        gone_x, gone_y, grad_tokens, grad_shift_attn, grad_scale_attn, qkv_sums = tie(
            gone_x, gone_y, grad_tokens, grad_shift_attn, grad_scale_attn, qkv_sums
        )
        rest = sum_last(column, gones, gone_x)
        column, gones = along_z(
            sum_third(qkv_x, gone_x, True, rest), sum_third(qkv_y, gone_y, False, rest)
        )
        grad_qkv = own_half(sum_last(column, gones, rest), core)
        mlp_part, grad_text = after((mlp_part, grad_text), gones[0])
        grad_kv2 = rest[:, : 2 * w_out.shape[1]]
        grad_out, grad_out2, grad_query2 = [
            own_half(part, core) for part in jnp.split(rest[:, grad_kv2.shape[1] :], 3, axis=1)
        ]
        here = mlp_part[:, : 2 * D].reshape(rows_here, 2, -1, rows_here).transpose(0, 2, 1, 3)
        here = here.reshape(rows_here, 2, -1, 2, rows_here)
        gone, mine = pick(here, other, 1), pick(here, core, 1)
        grad_fc1 = by_core(mine[:, :, None], pair(gone)[:, :, None], 2).reshape(w_fc1.shape)
        here = jnp.concatenate([mlp_part[:, 2 * D : 3 * D], mlp_part[:, 3 * D :]], axis=0)
        gone, mine = core_parts(here)
        gone, mine = own_half(gone, other), own_half(mine, core)
        grad_fc2 = by_core(mine, pair(gone), 0)
        fc1_sums = by_core(fc1_sums[0], fc1_sums[1], 1).reshape(2, 2, -1, rows_here)
        fc1_sums = fc1_sums.transpose(2, 0, 1, 3)
    else:
        grad_q, grad_kv1 = attend_backward(
            *self_qkv, grad_mixed1, attn_low, self_lse, 256, False, jnp.float32
        )
        grad_kv1 = lax.psum_scatter(grad_kv1, "seq", scatter_dimension=1, tiled=True)
        grad_qkv_low = flatten(jnp.concatenate([grad_q, low(grad_kv1)], axis=-1))
        grad_tokens, grad_shift_attn, grad_scale_attn, qkv_sums = attend_input(
            unflat(grad_qkv_low), wf_qkv, tokens, modulation[:, 1:2], grad_attn
        )
        grad_fc1 = scatter_plain(
            jnp.concatenate([low(dot_tn(flat_h, flatten(part))) for part in grads_pre], axis=1)
        )
        grad_fc2 = scatter_plain(
            jnp.concatenate([low(dot_tn(flatten(part), flat_gm)) for part in lows], axis=0)
        )
        grad_out2 = weight_grad(flatten(cross_low), grad_proj2)
        grad_kv2 = weight_grad(flatten(text), grad_kv)
        grad_query2 = weight_grad(flatten(after_low), grad_q2)
        grad_out = weight_grad(flatten(attn_low), grad_proj1)
        grad_qkv = weight_grad(flatten(h_attn), grad_qkv_low)
        fc1_sums = jnp.concatenate(fc1_sums, axis=1)
    grad_time = jnp.concatenate(
        [
            grad_shift_attn,
            grad_scale_attn,
            grad_gate_attn,
            grad_shift_mlp,
            grad_scale_mlp,
            grad_gate_mlp,
        ],
        axis=1,
    )
    qkv_sums = jnp.sum(qkv_sums, axis=0)
    grad_vectors = jnp.concatenate(
        [
            jnp.sum(grad_time, axis=0),
            qkv_sums[:, :D],
            qkv_sums[:, 2 * D :],
            column_sum(grad_proj1),
            column_sum(grad_q2),
            column_sum(grad_kv[:, D:]),
            jnp.sum(out2_sums, axis=0),
            jnp.sum(fc2_sums, axis=0),
            fc1_sums.reshape(-1, D),
        ],
        axis=0,
    ).T
    if swap:
        count = grad_vectors.shape[1]
        part = low(jnp.pad(grad_vectors, ((0, 0), (0, 128 - count))))
        part = low(part.astype(jnp.float32) + pair(part).astype(jnp.float32))
        blocks, gone = sum_first([part], True)
        sums, gone = sum_second(blocks, gone, True, part)
        part = sum_last(*along_z(sum_third(sums, gone, True, part)), part)
        grad_vectors = part[:, :count]
    else:
        grad_vectors = lax.psum_scatter(
            lax.psum(grad_vectors, "seq"), "fsdp", scatter_dimension=0, tiled=True
        )
    grad_time = grad_time.reshape(batch, 6 * D)
    if swap:
        grad_time = by_core(grad_time, pair(grad_time), 0)
        result, grad_tokens, grad_text = (
            trade_back(result), trade_back(grad_tokens), trade_back(grad_text),
        )
    else:
        grad_time = lax.psum(grad_time, "seq")
    return (
        result,
        grad_tokens,
        grad_time,
        grad_text,
        grad_vectors,
        grad_qkv,
        grad_out,
        grad_query2,
        grad_kv2,
        grad_out2,
        grad_fc1,
        grad_fc2,
    )


def solution(mesh):
    in_specs = (
        P("fsdp", "seq", None),
        P("fsdp", None),
        P("fsdp", "seq", None),
        P("fsdp", "seq", None),
        P("fsdp", None),
        P("fsdp", "seq"),
        P("fsdp", "seq"),
        P("fsdp", "seq"),
        P("fsdp", "seq"),
        P("fsdp", "seq"),
        P("fsdp", "seq"),
        P("fsdp", "seq"),
    )
    out_specs = (
        P("fsdp", "seq", None),
        P("fsdp", "seq", None),
        P("fsdp", None),
        P("fsdp", "seq", None),
        P("fsdp", None),
        P("fsdp", "seq"),
        P("fsdp", "seq"),
        P("fsdp", "seq"),
        P("fsdp", "seq"),
        P("fsdp", "seq"),
        P("fsdp", "seq"),
        P("fsdp", "seq"),
    )
    return jax.shard_map(body, mesh=mesh, in_specs=in_specs, out_specs=out_specs, check_vma=False)
```

time: 3000 us -> 782 us (0.26)
  waiting for transfers between devices: 2000 us -> 150 us
  matrix products: 541 us -> 110 us
  Pallas kernels: 0 us -> 268 us
  blocking collectives: 121 us -> 0 us
  local copies, waits for them, and re-layouts: 169 us -> 85.7 us
  other arithmetic: 140 us -> 57.3 us
  starting transfers between devices: 2.12 us -> 82.3 us
    unnamed x41 -> x1, waiting for transfers between devices: 828 us -> 0.02 us
    reduce_scatter x8 -> x0, waiting for transfers between devices: 653 us -> none  [the longest x1 317 us: body(): lax.psum_scatter(grad_terms[6], 'fsdp', scatter_dimension=0, tiled=True)]
    all_gather x11 -> x1, waiting for transfers between devices: 516 us -> 0.01 us  [body(): mlp_own = lax.all_gather(shard, 'fsdp', axis=0, tiled=True)]
    dot_general x66 -> x20, matrix products: 541 us -> 110 us  [the longest x14 72.9 us: dot_tn(): lax.dot_general(left, right, (((0,), (0,)), ((), ())), preferred_element_...]
    pallas_call x0 -> x17, Pallas kernels: none -> 268 us  [the longest x2 83.3 us: attend_backward(): pl.pallas_call(functools.partial(attend_backward_kernel, fused), grid=(ba...]
    ppermute x0 -> x79, waiting for transfers between devices: none -> 150 us  [the longest x6 37.5 us: column_pieces(): lax.ppermute(shard, 'fsdp', chip_shift(count, -step))]
    ppermute x0 -> x79, starting transfers between devices: none -> 82.3 us  [the longest x12 26 us: sum_last(): came = lax.ppermute(gone, 'fsdp', chip_shift(count, step))]
    all_gather x12 -> x0, blocking collectives: 68.4 us -> none  [the longest x1 43.4 us: gather_weights(): lax.all_gather(vectors, 'fsdp', axis=0, tiled=True)]
  transfers between devices with their start and end apart: 30 -> 80, of which waited for: 21 -> 24; matrix products, arithmetic and copies ran while one was open for 15% -> 20% of each run, Pallas kernels for 0% -> 30%
where the time goes in v1:
time: 782 us; the launch traced here: 770 us
  Pallas kernels  268 us (34%)
  waiting for transfers between devices  150 us (19%)
  matrix products  110 us (14%)
  local copies, waits for them, and re-layouts  85.7 us (11%)
  starting transfers between devices  82.3 us (11%)
  other arithmetic  57.3 us (7%)
  between operations  16.1 us (2%)
    pallas_call x2, Pallas kernels, attend_backward(): pl.pallas_call(functools.partial(attend_backward_kernel, fused), grid=(ba...  83.3 us
    dot_general x14, matrix products, dot_tn(): lax.dot_general(left, right, (((0,), (0,)), ((), ())), preferred_element_...  72.9 us
    ppermute x6, waiting for transfers between devices, column_pieces(): lax.ppermute(shard, 'fsdp', chip_shift(count, -step))  37.5 us
    ppermute x18, waiting for transfers between devices, across_chips(): came = lax.ppermute(gone, 'fsdp', chip_flip(lax.axis_size('fsdp'), bit))  35.2 us
    pallas_call x2, Pallas kernels, attend_forward(): pl.pallas_call(attend_forward_kernel, grid=(batch, rows // block), in_spe...  33.5 us
    unnamed x204, local copies, waits for them, and re-layouts  30 us
    ppermute x2, waiting for transfers between devices, near_pieces(): lax.ppermute(column, 'fsdp', chip_flip(count, 2))  28.4 us
    pallas_call x2, Pallas kernels, mlp_first(): pl.pallas_call(mlp_first_kernel, grid=(batch, 2 * D // MLP_TILE), in_spec...  28.1 us
  transfers between devices with their start and end apart: 80, of which 24 were waited for; matrix products, arithmetic and copies ran while one was open for 20% of the time, Pallas kernels for 30%

profile of v1, /device:TPU:0, one launch (start us, length us, event | category | flops | bytes accessed | tf_op | source)
XLA Modules:
  0.0 770.3 jit_solution(9070374554657882372)
XLA Ops:
  36.4 18.4 %collective-permute-done.1.refs_2_ = bf16[72,1728]{1,0:T(8,128)(2,1)S(1)} collective-permute-done((bf16[72,1728]{1,0:T(8,128)(2,1)S(1)}, bf16[72,1728]{1,0:T(8,128)(2,1)S(1)}, u32[]{:S(2)}, u32[]{:S(2)}) %collective-permute-start.1) | collective-permute-done | bytes 248864 | tf_op jit(solution)/shard_map/ppermute | solution.py:719
  54.9 6.3 collective-permute-start.8
  84.5 14.4 %collective-permute-done.13.refs_1_ = bf16[4,72,1728]{2,1,0:T(8,128)(2,1)} collective-permute-done((bf16[4,72,1728]{2,1,0:T(8,128)(2,1)S(1)}, bf16[4,72,1728]{2,1,0:T(8,128)(2,1)}, u32[]{:S(2)}, u32[]{:S(2)}) %collective-permute-start.13) | collective-permute-done | bytes 995360 | tf_op jit(solution)/shard_map/ppermute | solution.py:732
  101.6 6.0 collective-permute-done.14.refs_2_
  112.2 19.0 %collective-permute-done.18.refs_2_ = bf16[72,2880]{1,0:T(8,128)(2,1)} collective-permute-done((bf16[72,2880]{1,0:T(8,128)(2,1)}, bf16[72,2880]{1,0:T(8,128)(2,1)}, u32[]{:S(2)}, u32[]{:S(2)}) %collective-permute-start.18) | collective-permute-done | bytes 414752 | tf_op jit(solution)/shard_map/ppermute | solution.py:719
  141.0 7.3 shard_map.213
  148.3 15.1 %fusion.1.q_ref.k_ref.v_ref = bf16[1,1024,3456]{2,1,0:T(8,128)(2,1)} fusion(f32[3456]{0:T(1024)S(1)} %fusion.142, bf16[1152,3456]{1,0:T(8,128)(2,1)} %bitcast.352, bf16[1,1024,1152]{2,1,0:T(8,128)(2,1)} %fusion.7), kind=kOutput, calls=%fused_computation.9 | convolution fusion | flops 8160804864 | bytes 17413632 | tf_op jit(solution)/shard_map/dot_general | solution.py:72
  163.5 27.0 %shard_map.214 = (bf16[1,1024,1152]{2,1,0:T(8,128)(2,1)S(1)}, f32[1,16,1024]{2,1,0:T(8,128)S(1)}) custom-call(bf16[1,1024,3456]{2,1,0:T(8,128)(2,1)} %fusion.1.q_ref.k_ref.v_ref, bf16[1,1024,3456]{2,1,0:T(8,128)(2,1)} %fusion.1.q_ref.k_ref.v_ref, bf16[1,1024,3456]{2,1,0:T(8,128)(2,1)} %fusion.1.q_ref.k_ref.v_ref), custom_call_target="tpu_custom_call" | custom-call | flops 17179868 | bytes 9437 | tf_op jit(solution)/shard_map/pallas_call | solution.py:135
  190.5 14.0 %collective-permute-done.25.refs_1_ = bf16[4,72,2880]{2,1,0:T(8,128)(2,1)S(1)} collective-permute-done((bf16[4,72,2880]{2,1,0:T(8,128)(2,1)S(1)}, bf16[4,72,2880]{2,1,0:T(8,128)(2,1)S(1)}, u32[]{:S(2)}, u32[]{:S(2)}) %collective-permute-start.25) | collective-permute-done | bytes 1658912 | tf_op jit(solution)/shard_map/ppermute | solution.py:732
  207.3 18.8 %collective-permute-done.28.refs_4_ = bf16[4,72,1472]{2,1,0:T(8,128)(2,1)S(1)} collective-permute-done((bf16[4,72,1472]{2,1,0:T(8,128)(2,1)S(1)}, bf16[4,72,1472]{2,1,0:T(8,128)(2,1)S(1)}, u32[]{:S(2)}, u32[]{:S(2)}) %collective-permute-start.28) | collective-permute-done | bytes 847904 | tf_op jit(solution)/shard_map/ppermute | solution.py:741
  232.7 9.3 %shard_map.215 = (bf16[4,4,72,1152]{3,2,1,0:T(8,128)(2,1)}, bf16[4,4,72,1152]{3,2,1,0:T(8,128)(2,1)}, bf16[4,4,72,2304]{3,2,1,0:T(8,128)(2,1)}, bf16[4,4,72,1152]{3,2,1,0:T(8,128)(2,1)}) custom-call(s32[4]{0:T(128)S(1)} %pad_add_fusion.place, bf16[4,72,2880]{2,1,0:T(8,128)(2,1)S(1)} %shard_map.212.refs_0_, bf16[4,72,2880]{2,1,0:T(8,128)(2,1)} %copy-done.49, ...), custom_call_target="tpu_custom_call" | custom-call | bytes 26542 | tf_op jit(solution)/shard_map/pallas_call | solution.py:793
  242.0 11.3 %shard_map.216 = (f32[1,1024,1152]{2,1,0:T(8,128)}, f32[1,1024,1152]{2,1,0:T(8,128)}, bf16[1,1024,1152]{2,1,0:T(8,128)(2,1)S(1)}, bf16[1,1024,1152]{2,1,0:T(8,128)(2,1)S(1)}) custom-call(bf16[1,1024,1152]{2,1,0:T(8,128)(2,1)S(1)} %get-tuple-element.159.m_ref.o_ref, bf16[1152,1152]{1,0:T(8,128)(2,1)} %bitcast.380, f32[1,1152]{1,0:T(1,128)S(1)} %get-tuple-element.377.bo_ref, ...), custom_call_target="tpu_custom_call" | custom-call | flops 5435817 | bytes 24182 | tf_op jit(solution)/shard_map/pallas_call | solution.py:634
  255.5 6.5 shard_map.217
  264.9 5.4 shard_map.218
  277.0 14.0 %shard_map.219 = (bf16[1,1024,2304]{2,1,0:T(8,128)(2,1)}, bf16[1,1024,2304]{2,1,0:T(8,128)(2,1)}) custom-call(bf16[1,1024,1152]{2,1,0:T(8,128)(2,1)} %copy-done.9, bf16[1152,4608]{1,0:T(8,128)(2,1)} %all-gather.2.cloned.1.call-done.w_ref.wo_ref, f32[1,2304]{1,0:T(1,128)} %reshape.305.b_ref), custom_call_target="tpu_custom_call" | custom-call | flops 5435817 | bytes 17104 | tf_op jit(solution)/shard_map/pallas_call | solution.py:310
  292.0 14.1 %shard_map.220 = (bf16[1,1024,2304]{2,1,0:T(8,128)(2,1)}, bf16[1,1024,2304]{2,1,0:T(8,128)(2,1)}) custom-call(bf16[1,1024,1152]{2,1,0:T(8,128)(2,1)} %copy-done.9, bf16[1152,4608]{1,0:T(8,128)(2,1)} %collective-permute-done.34.w_ref.wc_ref, f32[1,2304]{1,0:T(1,128)} %reshape.306.b_ref), custom_call_target="tpu_custom_call" | custom-call | flops 5435817 | bytes 17104 | tf_op jit(solution)/shard_map/pallas_call | solution.py:310
  306.2 23.4 %shard_map.221 = (bf16[1,1024,1152]{2,1,0:T(8,128)(2,1)}, bf16[1,1024,1152]{2,1,0:T(8,128)(2,1)}, f32[1,1,1152]{2,1,0:T(1,128)}, f32[1,1,1152]{2,1,0:T(1,128)}) custom-call(bf16[1,1024,2304]{2,1,0:T(8,128)(2,1)} %get-tuple-element.174.lo_ref, bf16[1,1024,2304]{2,1,0:T(8,128)(2,1)} %get-tuple-element.176.lc_ref, ...), custom_call_target="tpu_custom_call" | custom-call | flops 10871635 | bytes 31850 | tf_op jit(solution)/shard_map/pallas_call | solution.py:379
  329.6 10.0 %convolution_convert_fusion.1 = bf16[2304,1152]{1,0:T(8,128)(2,1)} fusion(bf16[1,1024,2304]{2,1,0:T(8,128)(2,1)S(1)} %copy-done.39, bf16[1,1024,1152]{2,1,0:T(8,128)(2,1)} %get-tuple-element.188.g_ref), kind=kOutput, calls=%fused_computation.4 | convolution fusion | flops 5438472192 | bytes 12386304 | tf_op jit(solution)/shard_map/dot_general | solution.py:51
  342.1 9.7 %shard_map.222 = (bf16[1,1024,2304]{2,1,0:T(8,128)(2,1)S(1)}, f32[1,1,2304]{2,1,0:T(1,128)S(1)}) custom-call(bf16[1,1024,1152]{2,1,0:T(8,128)(2,1)S(1)} %copy-done.3, bf16[1152,4608]{1,0:T(8,128)(2,1)} %collective-permute-done.34.w_ref.wc_ref, bf16[1,1024,2304]{2,1,0:T(8,128)(2,1)S(1)} %copy-done.14), custom_call_target="tpu_custom_call" | custom-call | flops 5435817 | bytes 17104 | tf_op jit(solution)/shard_map/pallas_call | solution.py:426
  351.8 10.8 %fusion = bf16[2304,1152]{1,0:T(8,128)(2,1)S(1)} fusion(bf16[2304,1152]{1,0:T(8,128)(2,1)} %collective-permute-done.35, bf16[1,1024,2304]{2,1,0:T(8,128)(2,1)} %get-tuple-element.174.lo_ref, bf16[1,1024,1152]{2,1,0:T(8,128)(2,1)S(1)} %copy-done.3), kind=kOutput, calls=%fused_computation.2 | convolution fusion | flops 5443780608 | bytes 17694720 | tf_op jit(solution)/shard_map/dot_general | solution.py:51
  365.2 7.7 convolution_convert_fusion
  375.4 9.7 %shard_map.223 = (bf16[1,1024,2304]{2,1,0:T(8,128)(2,1)S(1)}, f32[1,1,2304]{2,1,0:T(1,128)S(1)}) custom-call(bf16[1,1024,1152]{2,1,0:T(8,128)(2,1)S(1)} %copy-done.3, bf16[1152,4608]{1,0:T(8,128)(2,1)} %all-gather.2.cloned.1.call-done.w_ref.wo_ref, bf16[1,1024,2304]{2,1,0:T(8,128)(2,1)S(1)} %bitcast.347), custom_call_target="tpu_custom_call" | custom-call | flops 5435817 | bytes 17104 | tf_op jit(solution)/shard_map/pallas_call | solution.py:426
  385.0 19.6 %collective-permute-done.37 = bf16[4,2,72,1152]{3,2,0,1:T(8,128)(2,1)} collective-permute-done((bf16[4,2,72,1152]{3,2,0,1:T(8,128)(2,1)S(1)}, bf16[4,2,72,1152]{3,2,0,1:T(8,128)(2,1)}, u32[]{:S(2)}, u32[]{:S(2)}) %collective-permute-start.37) | collective-permute-done | bytes 1327136 | tf_op jit(solution)/shard_map/ppermute | solution.py:850
  409.6 7.7 %add_convert_fusion.1 = bf16[1152,2304]{1,0:T(8,128)(2,1)S(1)} fusion(bf16[1152,2304]{1,0:T(8,128)(2,1)} %collective-permute-done.38, bf16[1,1024,2304]{2,1,0:T(8,128)(2,1)S(1)} %get-tuple-element.198.go_ref, bf16[1,1024,1152]{2,1,0:T(8,128)(2,1)S(1)} %copy-done.10), kind=kOutput, calls=%fused_computation.5 | convolution fusion | flops 5443780608 | bytes 17694720 | tf_op jit(solution)/shard_map/dot_general | solution.py:51
  420.6 25.1 %shard_map.224 = (f32[1,1024,1152]{2,1,0:T(8,128)}, bf16[1,1024,1152]{2,1,0:T(8,128)(2,1)}, f32[1,1,1152]{2,1,0:T(1,128)}, f32[1,1,1152]{2,1,0:T(1,128)}, f32[1,1,1152]{2,1,0:T(1,128)}) custom-call(bf16[1,1024,2304]{2,1,0:T(8,128)(2,1)} %copy-done.13, bf16[1,1024,2304]{2,1,0:T(8,128)(2,1)} %copy-done.12, ...), custom_call_target="tpu_custom_call" | custom-call | flops 10871635 | bytes 34209 | tf_op jit(solution)/shard_map/pallas_call | solution.py:514
  461.8 7.4 fusion.24.g_ref
  473.9 19.2 %shard_map.225 = (bf16[1,1024,1152]{2,1,0:T(8,128)(2,1)}, bf16[1,120,2304]{2,1,0:T(8,128)(2,1)}) custom-call(bf16[1,1024,1152]{2,1,0:T(8,128)(2,1)} %copy-done.6, bf16[1,120,2304]{2,1,0:T(8,128)(2,1)} %copy-done.2, bf16[1,120,2304]{2,1,0:T(8,128)(2,1)} %copy-done.2, bf16[1,1024,1152]{2,1,0:T(8,128)(2,1)} %fusion.24.g_ref, bf16[1,1024,1152]{2,1,0:T(8,128)(2,1)} %copy-done.7, ...), custom_call_target="tpu_custom_call" | custom-call | flops 5033164 | bytes 8460 | tf_op jit(solution)/shard_map/pallas_call | solution.py:241
  544.4 64.0 %shard_map.226 = bf16[1,1024,3456]{2,1,0:T(8,128)(2,1)} custom-call(bf16[1,1024,3456]{2,1,0:T(8,128)(2,1)} %fusion.1.q_ref.k_ref.v_ref, bf16[1,1024,3456]{2,1,0:T(8,128)(2,1)} %fusion.1.q_ref.k_ref.v_ref, bf16[1,1024,3456]{2,1,0:T(8,128)(2,1)} %fusion.1.q_ref.k_ref.v_ref, bf16[1,1024,1152]{2,1,0:T(8,128)(2,1)} %fusion.25.g_ref, ...), custom_call_target="tpu_custom_call" | custom-call | flops 42949672 | bytes 18874 | tf_op jit(solution)/shard_map/pallas_call | solution.py:241
  618.0 6.8 convolution_convert_fusion.2
  632.2 9.3 %add_convert_fusion.2 = bf16[1152,1792]{1,0:T(8,128)(2,1)S(1)} fusion(bf16[1152,1792]{1,0:T(8,128)(2,1)} %collective-permute-done.55, pred[]{:T(512)S(6)} %eq.80, bf16[1024,3456]{1,0:T(8,128)(2,1)} %bitcast.354, bf16[1,1024,1152]{2,1,0:T(8,128)(2,1)S(1)} %copy-done.60), kind=kOutput, calls=%fused_computation.6 | convolution fusion | flops 4235886592 | bytes 17956864 | tf_op jit(solution)/shard_map/dot_general | solution.py:51
  669.2 20.8 %shard_map.227 = (f32[1,1024,1152]{2,1,0:T(8,128)}, f32[1,1,1152]{2,1,0:T(1,128)}, f32[1,1,1152]{2,1,0:T(1,128)}, f32[1,1,3456]{2,1,0:T(1,128)}) custom-call(bf16[1,1024,3456]{2,1,0:T(8,128)(2,1)} %shard_map.226, bf16[1152,3456]{1,0:T(8,128)(2,1)} %bitcast.353, bf16[1,1024,1152]{2,1,0:T(8,128)(2,1)} %copy-done, f32[1,1,1152]{2,1,0:T(1,128)} %get-tuple-element.384.scale_ref, ...), custom_call_target="tpu_custom_call" | custom-call | flops 8153726 | bytes 26836 | tf_op jit(solution)/shard_map/pallas_call | solution.py:582
  717.2 10.0 %collective-permute-start.74 = (bf16[72,1792]{1,0:T(8,128)(2,1)}, bf16[72,1792]{1,0:T(8,128)(2,1)}, u32[]{:S(2)}, u32[]{:S(2)}) collective-permute-start(bf16[72,1792]{1,0:T(8,128)(2,1)} %get-tuple-element.356), channel_id=1, source_target_pairs={{0,8},{2,10},{4,12},{6,14},{8,16},{10,18},{12,20},{14,22},{16,24},... | collective-permute-start | bytes 774152 | tf_op jit(solution)/shard_map/ppermute | solution.py:876
  (533 shorter events, 286.0 us)
Async XLA Ops:
  7.2 268.2 %all-gather.2.cloned.1.call-start = ((), (), s32[]{:S(2)}) async-start(), calls=%async_computation | async-start | bytes 11280384 | tf_op jit(solution)/shard_map/all_gather | solution.py:994
  19.9 35.0 %collective-permute-start.1 = (bf16[72,1728]{1,0:T(8,128)(2,1)S(1)}, bf16[72,1728]{1,0:T(8,128)(2,1)S(1)}, u32[]{:S(2)}, u32[]{:S(2)}) collective-permute-start(bf16[72,1728]{1,0:T(8,128)(2,1)S(1)} %copy-done.17), channel_id=1, source_target_pairs={{0,16},{2,18},{4,20},{6,22},{8,24},{10,26},{12,28},{14,30},{16,0},... | collective-permute-start | bytes 746504 | tf_op jit(solution)/shard_map/ppermute | solution.py:719
  19.9 35.0 %collective-permute-start.2 = (bf16[72,1728]{1,0:T(8,128)(2,1)S(1)}, bf16[72,1728]{1,0:T(8,128)(2,1)S(1)}, u32[]{:S(2)}, u32[]{:S(2)}) collective-permute-start(bf16[72,1728]{1,0:T(8,128)(2,1)S(1)} %copy-done.17), channel_id=1, source_target_pairs={{0,8},{2,10},{4,12},{6,14},{8,16},{10,18},{12,20},{14,22},{16,24},... | collective-permute-start | bytes 746504 | tf_op jit(solution)/shard_map/ppermute | solution.py:719
  24.6 46.0 %collective-permute-start.12 = (bf16[1,512,1152]{2,1,0:T(8,128)(2,1)}, bf16[1,512,1152]{2,1,0:T(8,128)(2,1)}, u32[]{:S(2)}, u32[]{:S(2)}) collective-permute-start(bf16[1,512,1152]{2,1,0:T(8,128)(2,1)} %get-tuple-element.335), channel_id=1, source_target_pairs={{0,1},{1,0},{2,3},{3,2},{4,5},{5,4},{6,7},{7,6},{8,9},{9,8},{10,11... | collective-permute-start | bytes 3538952 | tf_op jit(solution)/shard_map/ppermute | solution.py:907
  36.4 37.1 %collective-permute-start.10 = (bf16[1,512,1152]{2,1,0:T(8,128)(2,1)S(1)}, bf16[1,512,1152]{2,1,0:T(8,128)(2,1)S(1)}, u32[]{:S(2)}, u32[]{:S(2)}) collective-permute-start(bf16[1,512,1152]{2,1,0:T(8,128)(2,1)S(1)} %get-tuple-element.337), channel_id=1, source_target_pairs={{0,1},{1,0},{2,3},{3,2},{4,5},{5,4},{6,7},{7,6},{8,9},{9,8},{10,11... | collective-permute-start | bytes 3538952 | tf_op jit(solution)/shard_map/ppermute | solution.py:907
  76.4 35.8 %collective-permute-start.17 = (bf16[72,2880]{1,0:T(8,128)(2,1)}, bf16[72,2880]{1,0:T(8,128)(2,1)}, u32[]{:S(2)}, u32[]{:S(2)}) collective-permute-start(bf16[72,2880]{1,0:T(8,128)(2,1)} %concatenate.122.refs_0_), channel_id=1, source_target_pairs={{0,24},{2,26},{4,28},{6,30},{8,0},{10,2},{12,4},{14,6},{16,8},{18,... | collective-permute-start | bytes 1244168 | tf_op jit(solution)/shard_map/ppermute | solution.py:719
  76.4 54.8 %collective-permute-start.18 = (bf16[72,2880]{1,0:T(8,128)(2,1)}, bf16[72,2880]{1,0:T(8,128)(2,1)}, u32[]{:S(2)}, u32[]{:S(2)}) collective-permute-start(bf16[72,2880]{1,0:T(8,128)(2,1)} %concatenate.122.refs_0_), channel_id=1, source_target_pairs={{0,16},{2,18},{4,20},{6,22},{8,24},{10,26},{12,28},{14,30},{16,0},... | collective-permute-start | bytes 1244168 | tf_op jit(solution)/shard_map/ppermute | solution.py:719
  78.4 52.8 %collective-permute-start.19 = (bf16[72,2880]{1,0:T(8,128)(2,1)}, bf16[72,2880]{1,0:T(8,128)(2,1)}, u32[]{:S(2)}, u32[]{:S(2)}) collective-permute-start(bf16[72,2880]{1,0:T(8,128)(2,1)} %concatenate.122.refs_0_), channel_id=1, source_target_pairs={{0,8},{2,10},{4,12},{6,14},{8,16},{10,18},{12,20},{14,22},{16,24},... | collective-permute-start | bytes 1244168 | tf_op jit(solution)/shard_map/ppermute | solution.py:719
  100.0 33.1 %collective-permute-start.15 = (bf16[4,72,896]{2,1,0:T(8,128)(2,1)S(1)}, bf16[4,72,896]{2,1,0:T(8,128)(2,1)S(1)}, u32[]{:S(2)}, u32[]{:S(2)}) collective-permute-start(bf16[4,72,896]{2,1,0:T(8,128)(2,1)S(1)} %slice.292), channel_id=1, source_target_pairs={{0,2},{2,0},{4,6},{6,4},{8,10},{10,8},{12,14},{14,12},{16,18},{18,... | collective-permute-start | bytes 1548296 | tf_op jit(solution)/shard_map/ppermute | solution.py:740
  136.7 67.8 %collective-permute-start.25 = (bf16[4,72,2880]{2,1,0:T(8,128)(2,1)S(1)}, bf16[4,72,2880]{2,1,0:T(8,128)(2,1)S(1)}, u32[]{:S(2)}, u32[]{:S(2)}) collective-permute-start(bf16[4,72,2880]{2,1,0:T(8,128)(2,1)S(1)} %shard_map.212.refs_0_), channel_id=1, source_target_pairs={{0,4},{2,6},{4,0},{6,2},{8,12},{10,14},{12,8},{14,10},{16,20},{18,... | collective-permute-start | bytes 4976648 | tf_op jit(solution)/shard_map/ppermute | solution.py:732
  138.2 66.3 %collective-permute-start.26 = (bf16[4,72,2880]{2,1,0:T(8,128)(2,1)S(1)}, bf16[4,72,2880]{2,1,0:T(8,128)(2,1)S(1)}, u32[]{:S(2)}, u32[]{:S(2)}) collective-permute-start(bf16[4,72,2880]{2,1,0:T(8,128)(2,1)S(1)} %shard_map.212.refs_0_), channel_id=1, source_target_pairs={{0,2},{2,0},{4,6},{6,4},{8,10},{10,8},{12,14},{14,12},{16,18},{18,... | collective-permute-start | bytes 4976648 | tf_op jit(solution)/shard_map/ppermute | solution.py:733
  372.9 36.8 %collective-permute-start.38 = (bf16[1152,2304]{1,0:T(8,128)(2,1)}, bf16[1152,2304]{1,0:T(8,128)(2,1)}, u32[]{:S(2)}, u32[]{:S(2)}) collective-permute-start(bf16[1152,2304]{1,0:T(8,128)(2,1)} %convolution_convert_fusion), channel_id=1, source_target_pairs={{0,1},{1,0},{2,3},{3,2},{4,5},{5,4},{6,7},{7,6},{8,9},{9,8},{10,11... | collective-permute-start | bytes 15925256 | tf_op jit(solution)/shard_map/ppermute | solution.py:921
  373.3 31.3 %collective-permute-start.37 = (bf16[4,2,72,1152]{3,2,0,1:T(8,128)(2,1)S(1)}, bf16[4,2,72,1152]{3,2,0,1:T(8,128)(2,1)}, u32[]{:S(2)}, u32[]{:S(2)}) collective-permute-start(bf16[4,2,72,1152]{3,2,0,1:T(8,128)(2,1)S(1)} %bitcast.394), channel_id=1, source_target_pairs={{0,4},{2,6},{4,0},{6,2},{8,12},{10,14},{12,8},{14,10},{16,20},{18,... | collective-permute-start | bytes 3981320 | tf_op jit(solution)/shard_map/ppermute | solution.py:850
  374.8 30.9 %collective-permute-start.36 = (bf16[4,2,72,1152]{3,2,0,1:T(8,128)(2,1)S(1)}, bf16[4,2,72,1152]{3,2,0,1:T(8,128)(2,1)S(1)}, u32[]{:S(2)}, u32[]{:S(2)}) collective-permute-start(bf16[4,2,72,1152]{3,2,0,1:T(8,128)(2,1)S(1)} %bitcast.395), channel_id=1, source_target_pairs={{0,2},{2,0},{4,6},{6,4},{8,10},{10,8},{12,14},{14,12},{16,18},{18,... | collective-permute-start | bytes 3981320 | tf_op jit(solution)/shard_map/ppermute | solution.py:850
  418.5 30.2 %collective-permute-start.41 = (bf16[4,2,72,1152]{3,2,0,1:T(8,128)(2,1)S(1)}, bf16[4,2,72,1152]{3,2,0,1:T(8,128)(2,1)}, u32[]{:S(2)}, u32[]{:S(2)}) collective-permute-start(bf16[4,2,72,1152]{3,2,0,1:T(8,128)(2,1)S(1)} %bitcast.393), channel_id=1, source_target_pairs={{0,4},{2,6},{4,0},{6,2},{8,12},{10,14},{12,8},{14,10},{16,20},{18,... | collective-permute-start | bytes 3981320 | tf_op jit(solution)/shard_map/ppermute | solution.py:850
  419.1 32.2 %collective-permute-start.40 = (bf16[4,2,72,1152]{3,2,0,1:T(8,128)(2,1)S(1)}, bf16[4,2,72,1152]{3,2,0,1:T(8,128)(2,1)S(1)}, u32[]{:S(2)}, u32[]{:S(2)}) collective-permute-start(bf16[4,2,72,1152]{3,2,0,1:T(8,128)(2,1)S(1)} %bitcast.392), channel_id=1, source_target_pairs={{0,2},{2,0},{4,6},{6,4},{8,10},{10,8},{12,14},{14,12},{16,18},{18,... | collective-permute-start | bytes 3981320 | tf_op jit(solution)/shard_map/ppermute | solution.py:850
  457.7 35.4 %collective-permute-start.45 = (bf16[4,72,1152]{2,1,0:T(8,128)(2,1)}, bf16[4,72,1152]{2,1,0:T(8,128)(2,1)S(1)}, u32[]{:S(2)}, u32[]{:S(2)}) collective-permute-start(bf16[4,72,1152]{2,1,0:T(8,128)(2,1)} %dynamic-slice_bitcast_fusion.8), channel_id=1, source_target_pairs={{0,4},{2,6},{4,0},{6,2},{8,12},{10,14},{12,8},{14,10},{16,20},{18,... | collective-permute-start | bytes 1990664 | tf_op jit(solution)/shard_map/ppermute | solution.py:850
  458.4 35.5 %collective-permute-start.46 = (bf16[4,72,1152]{2,1,0:T(8,128)(2,1)}, bf16[4,72,1152]{2,1,0:T(8,128)(2,1)}, u32[]{:S(2)}, u32[]{:S(2)}) collective-permute-start(bf16[4,72,1152]{2,1,0:T(8,128)(2,1)} %dynamic-slice_bitcast_fusion.7), channel_id=1, source_target_pairs={{0,2},{2,0},{4,6},{6,4},{8,10},{10,8},{12,14},{14,12},{16,18},{18,... | collective-permute-start | bytes 1990664 | tf_op jit(solution)/shard_map/ppermute | solution.py:850
  459.8 33.3 %collective-permute-start.42 = (bf16[4,72,1152]{2,1,0:T(8,128)(2,1)}, bf16[4,72,1152]{2,1,0:T(8,128)(2,1)}, u32[]{:S(2)}, u32[]{:S(2)}) collective-permute-start(bf16[4,72,1152]{2,1,0:T(8,128)(2,1)} %dynamic-slice_bitcast_fusion.6), channel_id=1, source_target_pairs={{0,4},{2,6},{4,0},{6,2},{8,12},{10,14},{12,8},{14,10},{16,20},{18,... | collective-permute-start | bytes 1990664 | tf_op jit(solution)/shard_map/ppermute | solution.py:850
  460.5 32.7 %collective-permute-start.44 = (bf16[4,72,1152]{2,1,0:T(8,128)(2,1)}, bf16[4,72,1152]{2,1,0:T(8,128)(2,1)}, u32[]{:S(2)}, u32[]{:S(2)}) collective-permute-start(bf16[4,72,1152]{2,1,0:T(8,128)(2,1)} %dynamic-slice_bitcast_fusion.5), channel_id=1, source_target_pairs={{0,2},{2,0},{4,6},{6,4},{8,10},{10,8},{12,14},{14,12},{16,18},{18,... | collective-permute-start | bytes 1990664 | tf_op jit(solution)/shard_map/ppermute | solution.py:850
  504.7 31.6 %collective-permute-start.47 = (bf16[1152,1152]{1,0:T(8,128)(2,1)S(1)}, bf16[1152,1152]{1,0:T(8,128)(2,1)S(1)}, u32[]{:S(2)}, u32[]{:S(2)}) collective-permute-start(bf16[1152,1152]{1,0:T(8,128)(2,1)S(1)} %convolution_convert_fusion.3), channel_id=1, source_target_pairs={{0,1},{1,0},{2,3},{3,2},{4,5},{5,4},{6,7},{7,6},{8,9},{9,8},{10,11... | collective-permute-start | bytes 7962632 | tf_op jit(solution)/shard_map/ppermute | solution.py:921
  514.7 93.8 %collective-permute-start.52 = (bf16[72,4608]{1,0:T(8,128)(2,1)}, bf16[72,4608]{1,0:T(8,128)(2,1)}, u32[]{:S(2)}, u32[]{:S(2)}) collective-permute-start(bf16[72,4608]{1,0:T(8,128)(2,1)} %get-tuple-element.227), channel_id=1, source_target_pairs={{0,8},{2,10},{4,12},{6,14},{8,16},{10,18},{12,20},{14,22},{16,24},... | collective-permute-start | bytes 1990664 | tf_op jit(solution)/shard_map/ppermute | solution.py:876
  516.2 92.3 %collective-permute-start.53 = (bf16[72,4608]{1,0:T(8,128)(2,1)}, bf16[72,4608]{1,0:T(8,128)(2,1)}, u32[]{:S(2)}, u32[]{:S(2)}) collective-permute-start(bf16[72,4608]{1,0:T(8,128)(2,1)} %get-tuple-element.229), channel_id=1, source_target_pairs={{0,16},{2,18},{4,20},{6,22},{8,24},{10,26},{12,28},{14,30},{16,0},... | collective-permute-start | bytes 1990664 | tf_op jit(solution)/shard_map/ppermute | solution.py:876
  524.5 84.0 %collective-permute-start.54 = (bf16[72,4608]{1,0:T(8,128)(2,1)}, bf16[72,4608]{1,0:T(8,128)(2,1)}, u32[]{:S(2)}, u32[]{:S(2)}) collective-permute-start(bf16[72,4608]{1,0:T(8,128)(2,1)} %get-tuple-element.231), channel_id=1, source_target_pairs={{0,24},{2,26},{4,28},{6,30},{8,0},{10,2},{12,4},{14,6},{16,8},{18,... | collective-permute-start | bytes 1990664 | tf_op jit(solution)/shard_map/ppermute | solution.py:876
  540.1 71.6 %collective-permute-start.51 = (bf16[4,2,72,1280]{3,2,0,1:T(8,128)(2,1)}, bf16[4,2,72,1280]{3,2,0,1:T(8,128)(2,1)}, u32[]{:S(2)}, u32[]{:S(2)}) collective-permute-start(bf16[4,2,72,1280]{3,2,0,1:T(8,128)(2,1)} %pad_maximum_fusion.4), channel_id=1, source_target_pairs={{0,4},{2,6},{4,0},{6,2},{8,12},{10,14},{12,8},{14,10},{16,20},{18,... | collective-permute-start | bytes 4423688 | tf_op jit(solution)/shard_map/ppermute | solution.py:850
  540.9 72.8 %collective-permute-start.50 = (bf16[4,2,72,1792]{3,2,0,1:T(8,128)(2,1)}, bf16[4,2,72,1792]{3,2,0,1:T(8,128)(2,1)}, u32[]{:S(2)}, u32[]{:S(2)}) collective-permute-start(bf16[4,2,72,1792]{3,2,0,1:T(8,128)(2,1)} %pad_maximum_fusion.3), channel_id=1, source_target_pairs={{0,2},{2,0},{4,6},{6,4},{8,10},{10,8},{12,14},{14,12},{16,18},{18,... | collective-permute-start | bytes 6193160 | tf_op jit(solution)/shard_map/ppermute | solution.py:850
  654.1 35.8 %collective-permute-start.59 = (bf16[4,2,72,896]{3,2,0,1:T(8,128)(2,1)}, bf16[4,2,72,896]{3,2,0,1:T(8,128)(2,1)S(1)}, u32[]{:S(2)}, u32[]{:S(2)}) collective-permute-start(bf16[4,2,72,896]{3,2,0,1:T(8,128)(2,1)} %bitcast.334), channel_id=1, source_target_pairs={{0,4},{2,6},{4,0},{6,2},{8,12},{10,14},{12,8},{14,10},{16,20},{18,... | collective-permute-start | bytes 3096584 | tf_op jit(solution)/shard_map/ppermute | solution.py:850
  655.4 35.0 %collective-permute-start.58 = (bf16[4,2,72,896]{3,2,0,1:T(8,128)(2,1)}, bf16[4,2,72,896]{3,2,0,1:T(8,128)(2,1)}, u32[]{:S(2)}, u32[]{:S(2)}) collective-permute-start(bf16[4,2,72,896]{3,2,0,1:T(8,128)(2,1)} %bitcast.335), channel_id=1, source_target_pairs={{0,2},{2,0},{4,6},{6,4},{8,10},{10,8},{12,14},{14,12},{16,18},{18,... | collective-permute-start | bytes 3096584 | tf_op jit(solution)/shard_map/ppermute | solution.py:850
  665.3 29.9 %collective-permute-start.63 = (bf16[72,3072]{1,0:T(8,128)(2,1)}, bf16[72,3072]{1,0:T(8,128)(2,1)S(1)}, u32[]{:S(2)}, u32[]{:S(2)}) collective-permute-start(bf16[72,3072]{1,0:T(8,128)(2,1)} %get-tuple-element.256), channel_id=1, source_target_pairs={{0,8},{2,10},{4,12},{6,14},{8,16},{10,18},{12,20},{14,22},{16,24},... | collective-permute-start | bytes 1327112 | tf_op jit(solution)/shard_map/ppermute | solution.py:876
  665.3 31.7 %collective-permute-start.64 = (bf16[72,3072]{1,0:T(8,128)(2,1)}, bf16[72,3072]{1,0:T(8,128)(2,1)}, u32[]{:S(2)}, u32[]{:S(2)}) collective-permute-start(bf16[72,3072]{1,0:T(8,128)(2,1)} %get-tuple-element.258), channel_id=1, source_target_pairs={{0,16},{2,18},{4,20},{6,22},{8,24},{10,26},{12,28},{14,30},{16,0},... | collective-permute-start | bytes 1327112 | tf_op jit(solution)/shard_map/ppermute | solution.py:876
  666.3 30.8 %collective-permute-start.65 = (bf16[72,3072]{1,0:T(8,128)(2,1)}, bf16[72,3072]{1,0:T(8,128)(2,1)}, u32[]{:S(2)}, u32[]{:S(2)}) collective-permute-start(bf16[72,3072]{1,0:T(8,128)(2,1)} %get-tuple-element.260), channel_id=1, source_target_pairs={{0,24},{2,26},{4,28},{6,30},{8,0},{10,2},{12,4},{14,6},{16,8},{18,... | collective-permute-start | bytes 1327112 | tf_op jit(solution)/shard_map/ppermute | solution.py:876
  703.6 54.5 %collective-permute-start.60 = (f32[1,512,1152]{2,1,0:T(8,128)}, f32[1,512,1152]{2,1,0:T(8,128)}, u32[]{:S(2)}, u32[]{:S(2)}) collective-permute-start(f32[1,512,1152]{2,1,0:T(8,128)} %get-tuple-element.316), channel_id=1, source_target_pairs={{0,1},{1,0},{2,3},{3,2},{4,5},{5,4},{6,7},{7,6},{8,9},{9,8},{10,11... | collective-permute-start | bytes 7077896 | tf_op jit(solution)/shard_map/ppermute | solution.py:921
  (146 other events, 1728.8 us)
Sparse Core Ops, SparseCore 0:
  15.2 206.1 all-gather.1

commit v2 on v1

--- a/solution.py
+++ b/solution.py
@@ -1058,6 +1058,33 @@
         lows, mlp, vec[12:13], after_cross, modulation[:, 5:6], cotangent
     )
 
+    def small_sums():
+        grad_time = jnp.concatenate(
+            [
+                grad_shift_attn,
+                grad_scale_attn,
+                grad_gate_attn,
+                grad_shift_mlp,
+                grad_scale_mlp,
+                grad_gate_mlp,
+            ],
+            axis=1,
+        )
+        qkv_rows_sum = jnp.sum(qkv_sums, axis=0)
+        grad_vectors = jnp.concatenate(
+            [
+                jnp.sum(grad_time, axis=0),
+                qkv_rows_sum[:, :D],
+                qkv_rows_sum[:, 2 * D :],
+                *small[1:],
+                jnp.sum(out2_sums, axis=0),
+                jnp.sum(fc2_sums, axis=0),
+                fc1_sums.reshape(-1, D),
+            ],
+            axis=0,
+        ).T
+        return grad_time, grad_vectors
+
     flat_h, flat_gm = flatten(h_mlp), flatten(grad_mlp)
     if swap:
         own_low, other_low = flatten(lows[0]), flatten(lows[1])
@@ -1073,13 +1100,14 @@
         sent = low(dot_tn(flat_h, flatten(other_pre)))
         sent, grad_mlp = tie(sent, grad_mlp)
         own_pre, own_sums = mlp_slope(grad_mlp, mlp[0], hidden[0][1])
-        fc2_x, fc2_gone_x = sum_second(fc2_x, fc2_gone_x, True, own_pre)
-        fc2_y, fc2_gone_y = sum_second(fc2_y, fc2_gone_y, False, own_pre)
-        fc2_gone_x, fc2_gone_y, own_pre = tie(fc2_gone_x, fc2_gone_y, own_pre)
         fc1_part = low(dot_tn(flat_h, flatten(own_pre)) + pair(sent).astype(jnp.float32))
         fc1_x, fc1_gone_x = sum_first([fc1_part[:, :D]], True)
         fc1_y, fc1_gone_y = sum_first([fc1_part[:, D:]], False)
-        own_pre, fc1_gone_x, fc1_gone_y = tie(own_pre, fc1_gone_x, fc1_gone_y)
+        fc2_x, fc2_gone_x = sum_second(fc2_x, fc2_gone_x, True, fc1_gone_x)
+        fc2_y, fc2_gone_y = sum_second(fc2_y, fc2_gone_y, False, fc1_gone_y)
+        own_pre, fc1_gone_x, fc1_gone_y, fc2_gone_x, fc2_gone_y = tie(
+            own_pre, fc1_gone_x, fc1_gone_y, fc2_gone_x, fc2_gone_y
+        )
         result = after(result, fc1_gone_x)
         grads_pre, fc1_sums = [own_pre, other_pre], [own_sums, other_sums]
     else:
@@ -1087,6 +1115,9 @@
         grads_pre = [grad_pre for grad_pre, _ in slopes]
         fc1_sums = [sums for _, sums in slopes]
     fc1_sums = [jnp.sum(sums, axis=0) for sums in fc1_sums]
+    if swap:
+        fc1_sums = by_core(fc1_sums[0], fc1_sums[1], 1).reshape(2, 2, -1, rows_here)
+        fc1_sums = fc1_sums.transpose(2, 0, 1, 3)
     grad_cross, grad_proj2, grad_shift_mlp, grad_scale_mlp, out2_sums = mlp_input(
         grads_pre, mlp, after_cross, modulation[:, 4:5], cotangent
     )
@@ -1130,7 +1161,9 @@
         rest_y, gone_y = sum_first(
             [out2_part, pair_grad(flatten(after_low), grad_q2)], False
         )
-        gone_x, gone_y, grad_mixed1 = tie(gone_x, gone_y, grad_mixed1)
+        small = (grad_text, column_sum(grad_proj1), column_sum(grad_q2), column_sum(grad_kv[:, D:]))
+        gone_x, gone_y, grad_mixed1, small = tie(gone_x, gone_y, grad_mixed1, small)
+        grad_text = small[0]
         (grad_qkv_low,) = attend_backward(
             *self_qkv, grad_mixed1, attn_low, self_lse, 256, True, jnp.bfloat16
         )
@@ -1159,10 +1192,20 @@
             gone_x, gone_y, grad_tokens, grad_shift_attn, grad_scale_attn, qkv_sums
         )
         rest = sum_last(column, gones, gone_x)
+        grad_time, grad_vectors = small_sums()
+        count = grad_vectors.shape[1]
+        part = low(jnp.pad(grad_vectors, ((0, 0), (0, 128 - count))))
+        part = low(part.astype(jnp.float32) + pair(part).astype(jnp.float32))
+        blocks, gone = sum_first([part], True)
+        sums, gone = sum_second(blocks, gone, True, part)
+        grad_tokens = trade_back(grad_tokens)
         column, gones = along_z(
-            sum_third(qkv_x, gone_x, True, rest), sum_third(qkv_y, gone_y, False, rest)
+            sum_third(qkv_x, gone_x, True, grad_tokens),
+            sum_third(qkv_y, gone_y, False, grad_tokens),
         )
         grad_qkv = own_half(sum_last(column, gones, rest), core)
+        vec_column, vec_gones = along_z(sum_third(sums, gone, True, gones[0]))
+        grad_vectors = sum_last(vec_column, vec_gones, rest)[:, :count]
         mlp_part, grad_text = after((mlp_part, grad_text), gones[0])
         grad_kv2 = rest[:, : 2 * w_out.shape[1]]
         grad_out, grad_out2, grad_query2 = [
@@ -1176,8 +1219,6 @@
         gone, mine = core_parts(here)
         gone, mine = own_half(gone, other), own_half(mine, core)
         grad_fc2 = by_core(mine, pair(gone), 0)
-        fc1_sums = by_core(fc1_sums[0], fc1_sums[1], 1).reshape(2, 2, -1, rows_here)
-        fc1_sums = fc1_sums.transpose(2, 0, 1, 3)
     else:
         grad_q, grad_kv1 = attend_backward(
             *self_qkv, grad_mixed1, attn_low, self_lse, 256, False, jnp.float32
@@ -1199,50 +1240,15 @@
         grad_out = weight_grad(flatten(attn_low), grad_proj1)
         grad_qkv = weight_grad(flatten(h_attn), grad_qkv_low)
         fc1_sums = jnp.concatenate(fc1_sums, axis=1)
-    grad_time = jnp.concatenate(
-        [
-            grad_shift_attn,
-            grad_scale_attn,
-            grad_gate_attn,
-            grad_shift_mlp,
-            grad_scale_mlp,
-            grad_gate_mlp,
-        ],
-        axis=1,
-    )
-    qkv_sums = jnp.sum(qkv_sums, axis=0)
-    grad_vectors = jnp.concatenate(
-        [
-            jnp.sum(grad_time, axis=0),
-            qkv_sums[:, :D],
-            qkv_sums[:, 2 * D :],
-            column_sum(grad_proj1),
-            column_sum(grad_q2),
-            column_sum(grad_kv[:, D:]),
-            jnp.sum(out2_sums, axis=0),
-            jnp.sum(fc2_sums, axis=0),
-            fc1_sums.reshape(-1, D),
-        ],
-        axis=0,
-    ).T
-    if swap:
-        count = grad_vectors.shape[1]
-        part = low(jnp.pad(grad_vectors, ((0, 0), (0, 128 - count))))
-        part = low(part.astype(jnp.float32) + pair(part).astype(jnp.float32))
-        blocks, gone = sum_first([part], True)
-        sums, gone = sum_second(blocks, gone, True, part)
-        part = sum_last(*along_z(sum_third(sums, gone, True, part)), part)
-        grad_vectors = part[:, :count]
-    else:
+        small = (grad_text, column_sum(grad_proj1), column_sum(grad_q2), column_sum(grad_kv[:, D:]))
+        grad_time, grad_vectors = small_sums()
         grad_vectors = lax.psum_scatter(
             lax.psum(grad_vectors, "seq"), "fsdp", scatter_dimension=0, tiled=True
         )
     grad_time = grad_time.reshape(batch, 6 * D)
     if swap:
         grad_time = by_core(grad_time, pair(grad_time), 0)
-        result, grad_tokens, grad_text = (
-            trade_back(result), trade_back(grad_tokens), trade_back(grad_text),
-        )
+        result, grad_text = trade_back(result), trade_back(grad_text)
     else:
         grad_time = lax.psum(grad_time, "seq")
     return (

time: 782 us -> 781 us (level)
  waiting for transfers between devices: 150 us -> 167 us
  starting transfers between devices: 82.3 us -> 72 us
    ppermute x12, waiting for transfers between devices: 4.91 us -> 19.1 us  [sum_last(): came = lax.ppermute(gone, 'fsdp', chip_shift(count, step))]
    ppermute x12, starting transfers between devices: 26 us -> 16.4 us  [sum_last(): came = lax.ppermute(gone, 'fsdp', chip_shift(count, step))]
    unnamed x204 -> x200, local copies, waits for them, and re-layouts: 30 us -> 32.6 us
  transfers between devices with their start and end apart: 80 -> 80, of which waited for: 24 -> 22; matrix products, arithmetic and copies ran while one was open for 20% -> 19% of each run, Pallas kernels for 30% -> 30%
where the time goes in v2:
time: 781 us; the launch traced here: 773 us
  Pallas kernels  269 us (34%)
  waiting for transfers between devices  167 us (21%)
  matrix products  108 us (14%)
  local copies, waits for them, and re-layouts  84.2 us (11%)
  starting transfers between devices  72 us (9%)
  other arithmetic  56.8 us (7%)
  between operations  16.1 us (2%)
    pallas_call x2, Pallas kernels, attend_backward(): pl.pallas_call(functools.partial(attend_backward_kernel, fused), grid=(ba...  83.3 us
    dot_general x14, matrix products, dot_tn(): lax.dot_general(left, right, (((0,), (0,)), ((), ())), preferred_element_...  71.7 us
    ppermute x6, waiting for transfers between devices, column_pieces(): lax.ppermute(shard, 'fsdp', chip_shift(count, -step))  40.9 us
    pallas_call x2, Pallas kernels, attend_forward(): pl.pallas_call(attend_forward_kernel, grid=(batch, rows // block), in_spe...  33.5 us
    unnamed x200, local copies, waits for them, and re-layouts  32.6 us
    ppermute x2, waiting for transfers between devices, near_pieces(): lax.ppermute(column, 'fsdp', chip_flip(count, 2))  31.5 us
    ppermute x18, waiting for transfers between devices, across_chips(): came = lax.ppermute(gone, 'fsdp', chip_flip(lax.axis_size('fsdp'), bit))  28.1 us
    pallas_call x2, Pallas kernels, mlp_first(): pl.pallas_call(mlp_first_kernel, grid=(batch, 2 * D // MLP_TILE), in_spec...  27.9 us
  transfers between devices with their start and end apart: 80, of which 22 were waited for; matrix products, arithmetic and copies ran while one was open for 19% of the time, Pallas kernels for 30%

profile of v2, /device:TPU:0, one launch (start us, length us, event | category | flops | bytes accessed | tf_op | source)
XLA Modules:
  0.0 772.7 jit_solution(3312807943304048135)
XLA Ops:
  36.4 21.8 %collective-permute-done.1.refs_2_ = bf16[72,1728]{1,0:T(8,128)(2,1)S(1)} collective-permute-done((bf16[72,1728]{1,0:T(8,128)(2,1)S(1)}, bf16[72,1728]{1,0:T(8,128)(2,1)S(1)}, u32[]{:S(2)}, u32[]{:S(2)}) %collective-permute-start.1) | collective-permute-done | bytes 248864 | tf_op jit(solution)/shard_map/ppermute | solution.py:719
  85.7 13.5 %collective-permute-done.13.refs_1_ = bf16[4,72,1728]{2,1,0:T(8,128)(2,1)} collective-permute-done((bf16[4,72,1728]{2,1,0:T(8,128)(2,1)S(1)}, bf16[4,72,1728]{2,1,0:T(8,128)(2,1)}, u32[]{:S(2)}, u32[]{:S(2)}) %collective-permute-start.13) | collective-permute-done | bytes 995360 | tf_op jit(solution)/shard_map/ppermute | solution.py:732
  101.8 8.5 %collective-permute-done.14.refs_2_ = bf16[4,72,1728]{2,1,0:T(8,128)(2,1)} collective-permute-done((bf16[4,72,1728]{2,1,0:T(8,128)(2,1)S(1)}, bf16[4,72,1728]{2,1,0:T(8,128)(2,1)}, u32[]{:S(2)}, u32[]{:S(2)}) %collective-permute-start.14) | collective-permute-done | bytes 995360 | tf_op jit(solution)/shard_map/ppermute | solution.py:733
  115.0 19.1 %collective-permute-done.18.refs_2_ = bf16[72,2880]{1,0:T(8,128)(2,1)} collective-permute-done((bf16[72,2880]{1,0:T(8,128)(2,1)}, bf16[72,2880]{1,0:T(8,128)(2,1)}, u32[]{:S(2)}, u32[]{:S(2)}) %collective-permute-start.18) | collective-permute-done | bytes 414752 | tf_op jit(solution)/shard_map/ppermute | solution.py:719
  143.7 7.3 shard_map.213
  151.0 15.2 %fusion.1.q_ref.k_ref.v_ref = bf16[1,1024,3456]{2,1,0:T(8,128)(2,1)} fusion(f32[3456]{0:T(1024)S(1)} %fusion.141, bf16[1152,3456]{1,0:T(8,128)(2,1)} %bitcast.355, bf16[1,1024,1152]{2,1,0:T(8,128)(2,1)} %fusion.7), kind=kOutput, calls=%fused_computation.9 | convolution fusion | flops 8160804864 | bytes 17413632 | tf_op jit(solution)/shard_map/dot_general | solution.py:72
  166.2 27.0 %shard_map.214 = (bf16[1,1024,1152]{2,1,0:T(8,128)(2,1)S(1)}, f32[1,16,1024]{2,1,0:T(8,128)S(1)}) custom-call(bf16[1,1024,3456]{2,1,0:T(8,128)(2,1)} %fusion.1.q_ref.k_ref.v_ref, bf16[1,1024,3456]{2,1,0:T(8,128)(2,1)} %fusion.1.q_ref.k_ref.v_ref, bf16[1,1024,3456]{2,1,0:T(8,128)(2,1)} %fusion.1.q_ref.k_ref.v_ref), custom_call_target="tpu_custom_call" | custom-call | flops 17179868 | bytes 9437 | tf_op jit(solution)/shard_map/pallas_call | solution.py:135
  193.2 18.0 %collective-permute-done.25.refs_1_ = bf16[4,72,2880]{2,1,0:T(8,128)(2,1)S(1)} collective-permute-done((bf16[4,72,2880]{2,1,0:T(8,128)(2,1)S(1)}, bf16[4,72,2880]{2,1,0:T(8,128)(2,1)S(1)}, u32[]{:S(2)}, u32[]{:S(2)}) %collective-permute-start.25) | collective-permute-done | bytes 1658912 | tf_op jit(solution)/shard_map/ppermute | solution.py:732
  214.0 18.7 %collective-permute-done.28.refs_4_ = bf16[4,72,1472]{2,1,0:T(8,128)(2,1)S(1)} collective-permute-done((bf16[4,72,1472]{2,1,0:T(8,128)(2,1)S(1)}, bf16[4,72,1472]{2,1,0:T(8,128)(2,1)S(1)}, u32[]{:S(2)}, u32[]{:S(2)}) %collective-permute-start.28) | collective-permute-done | bytes 847904 | tf_op jit(solution)/shard_map/ppermute | solution.py:741
  239.3 9.3 %shard_map.215 = (bf16[4,4,72,1152]{3,2,1,0:T(8,128)(2,1)}, bf16[4,4,72,1152]{3,2,1,0:T(8,128)(2,1)}, bf16[4,4,72,2304]{3,2,1,0:T(8,128)(2,1)}, bf16[4,4,72,1152]{3,2,1,0:T(8,128)(2,1)}) custom-call(s32[4]{0:T(128)S(1)} %pad_add_fusion.place, bf16[4,72,2880]{2,1,0:T(8,128)(2,1)S(1)} %shard_map.212.refs_0_, bf16[4,72,2880]{2,1,0:T(8,128)(2,1)} %copy-done.46, ...), custom_call_target="tpu_custom_call" | custom-call | bytes 26542 | tf_op jit(solution)/shard_map/pallas_call | solution.py:793
  248.6 11.3 %shard_map.216 = (f32[1,1024,1152]{2,1,0:T(8,128)}, f32[1,1024,1152]{2,1,0:T(8,128)}, bf16[1,1024,1152]{2,1,0:T(8,128)(2,1)S(1)}, bf16[1,1024,1152]{2,1,0:T(8,128)(2,1)S(1)}) custom-call(bf16[1,1024,1152]{2,1,0:T(8,128)(2,1)S(1)} %get-tuple-element.162.m_ref.o_ref, bf16[1152,1152]{1,0:T(8,128)(2,1)} %bitcast.385, f32[1,1152]{1,0:T(1,128)S(1)} %get-tuple-element.383.bo_ref, ...), custom_call_target="tpu_custom_call" | custom-call | flops 5435817 | bytes 24182 | tf_op jit(solution)/shard_map/pallas_call | solution.py:634
  262.1 6.5 shard_map.217
  283.6 13.9 %shard_map.219 = (bf16[1,1024,2304]{2,1,0:T(8,128)(2,1)}, bf16[1,1024,2304]{2,1,0:T(8,128)(2,1)}) custom-call(bf16[1,1024,1152]{2,1,0:T(8,128)(2,1)} %copy-done.9, bf16[1152,4608]{1,0:T(8,128)(2,1)} %all-gather.2.cloned.1.call-done.w_ref.wo_ref, f32[1,2304]{1,0:T(1,128)} %reshape.305.b_ref), custom_call_target="tpu_custom_call" | custom-call | flops 5435817 | bytes 17104 | tf_op jit(solution)/shard_map/pallas_call | solution.py:310
  298.6 14.0 %shard_map.220 = (bf16[1,1024,2304]{2,1,0:T(8,128)(2,1)}, bf16[1,1024,2304]{2,1,0:T(8,128)(2,1)}) custom-call(bf16[1,1024,1152]{2,1,0:T(8,128)(2,1)} %copy-done.9, bf16[1152,4608]{1,0:T(8,128)(2,1)} %collective-permute-done.34.w_ref.wc_ref, f32[1,2304]{1,0:T(1,128)} %reshape.306.b_ref), custom_call_target="tpu_custom_call" | custom-call | flops 5435817 | bytes 17104 | tf_op jit(solution)/shard_map/pallas_call | solution.py:310
  312.6 23.4 %shard_map.221 = (bf16[1,1024,1152]{2,1,0:T(8,128)(2,1)}, bf16[1,1024,1152]{2,1,0:T(8,128)(2,1)}, f32[1,1,1152]{2,1,0:T(1,128)}, f32[1,1,1152]{2,1,0:T(1,128)}) custom-call(bf16[1,1024,2304]{2,1,0:T(8,128)(2,1)} %get-tuple-element.177.lo_ref, bf16[1,1024,2304]{2,1,0:T(8,128)(2,1)} %get-tuple-element.179.lc_ref, ...), custom_call_target="tpu_custom_call" | custom-call | flops 10871635 | bytes 31850 | tf_op jit(solution)/shard_map/pallas_call | solution.py:379
  336.0 10.1 %convolution_convert_fusion.1 = bf16[2304,1152]{1,0:T(8,128)(2,1)} fusion(bf16[1,1024,2304]{2,1,0:T(8,128)(2,1)S(1)} %copy-done.38, bf16[1,1024,1152]{2,1,0:T(8,128)(2,1)} %get-tuple-element.190.g_ref), kind=kOutput, calls=%fused_computation.4 | convolution fusion | flops 5438472192 | bytes 12386304 | tf_op jit(solution)/shard_map/dot_general | solution.py:51
  348.6 9.7 %shard_map.222 = (bf16[1,1024,2304]{2,1,0:T(8,128)(2,1)S(1)}, f32[1,1,2304]{2,1,0:T(1,128)S(1)}) custom-call(bf16[1,1024,1152]{2,1,0:T(8,128)(2,1)S(1)} %copy-done.3, bf16[1152,4608]{1,0:T(8,128)(2,1)} %collective-permute-done.34.w_ref.wc_ref, bf16[1,1024,2304]{2,1,0:T(8,128)(2,1)S(1)} %copy-done.14), custom_call_target="tpu_custom_call" | custom-call | flops 5435817 | bytes 17104 | tf_op jit(solution)/shard_map/pallas_call | solution.py:426
  358.2 10.8 %fusion = bf16[2304,1152]{1,0:T(8,128)(2,1)S(1)} fusion(bf16[2304,1152]{1,0:T(8,128)(2,1)} %collective-permute-done.35, bf16[1,1024,2304]{2,1,0:T(8,128)(2,1)} %get-tuple-element.177.lo_ref, bf16[1,1024,1152]{2,1,0:T(8,128)(2,1)S(1)} %copy-done.3), kind=kOutput, calls=%fused_computation.2 | convolution fusion | flops 5443780608 | bytes 17694720 | tf_op jit(solution)/shard_map/dot_general | solution.py:51
  373.3 7.7 convolution_convert_fusion
  383.5 9.7 %shard_map.223 = (bf16[1,1024,2304]{2,1,0:T(8,128)(2,1)S(1)}, f32[1,1,2304]{2,1,0:T(1,128)S(1)}) custom-call(bf16[1,1024,1152]{2,1,0:T(8,128)(2,1)S(1)} %copy-done.3, bf16[1152,4608]{1,0:T(8,128)(2,1)} %all-gather.2.cloned.1.call-done.w_ref.wo_ref, bf16[1,1024,2304]{2,1,0:T(8,128)(2,1)S(1)} %bitcast.348), custom_call_target="tpu_custom_call" | custom-call | flops 5435817 | bytes 17104 | tf_op jit(solution)/shard_map/pallas_call | solution.py:426
  393.2 9.1 %add_convert_fusion.1 = bf16[1152,2304]{1,0:T(8,128)(2,1)S(1)} fusion(bf16[1152,2304]{1,0:T(8,128)(2,1)} %collective-permute-done.36, bf16[1,1024,2304]{2,1,0:T(8,128)(2,1)S(1)} %get-tuple-element.200.go_ref, bf16[1,1024,1152]{2,1,0:T(8,128)(2,1)S(1)} %copy-done.10), kind=kOutput, calls=%fused_computation.5 | convolution fusion | flops 5443780608 | bytes 17694720 | tf_op jit(solution)/shard_map/dot_general | solution.py:51
  403.4 9.5 %collective-permute-done.37 = bf16[4,2,72,1152]{3,2,0,1:T(8,128)(2,1)} collective-permute-done((bf16[4,2,72,1152]{3,2,0,1:T(8,128)(2,1)}, bf16[4,2,72,1152]{3,2,0,1:T(8,128)(2,1)}, u32[]{:S(2)}, u32[]{:S(2)}) %collective-permute-start.37) | collective-permute-done | bytes 1327136 | tf_op jit(solution)/shard_map/ppermute | solution.py:850
  420.6 25.1 %shard_map.224 = (f32[1,1024,1152]{2,1,0:T(8,128)}, bf16[1,1024,1152]{2,1,0:T(8,128)(2,1)}, f32[1,1,1152]{2,1,0:T(1,128)}, f32[1,1,1152]{2,1,0:T(1,128)}, f32[1,1,1152]{2,1,0:T(1,128)}) custom-call(bf16[1,1024,2304]{2,1,0:T(8,128)(2,1)} %copy-done.13, bf16[1,1024,2304]{2,1,0:T(8,128)(2,1)} %copy-done.12, ...), custom_call_target="tpu_custom_call" | custom-call | flops 10871635 | bytes 34209 | tf_op jit(solution)/shard_map/pallas_call | solution.py:514
  462.0 7.4 fusion.24.g_ref
  474.0 19.3 %shard_map.225 = (bf16[1,1024,1152]{2,1,0:T(8,128)(2,1)}, bf16[1,120,2304]{2,1,0:T(8,128)(2,1)}) custom-call(bf16[1,1024,1152]{2,1,0:T(8,128)(2,1)} %copy-done.6, bf16[1,120,2304]{2,1,0:T(8,128)(2,1)} %copy-done.2, bf16[1,120,2304]{2,1,0:T(8,128)(2,1)} %copy-done.2, bf16[1,1024,1152]{2,1,0:T(8,128)(2,1)} %fusion.24.g_ref, bf16[1,1024,1152]{2,1,0:T(8,128)(2,1)} %copy-done.7, ...), custom_call_target="tpu_custom_call" | custom-call | flops 5033164 | bytes 8460 | tf_op jit(solution)/shard_map/pallas_call | solution.py:241
  546.1 64.0 %shard_map.226 = bf16[1,1024,3456]{2,1,0:T(8,128)(2,1)} custom-call(bf16[1,1024,3456]{2,1,0:T(8,128)(2,1)} %fusion.1.q_ref.k_ref.v_ref, bf16[1,1024,3456]{2,1,0:T(8,128)(2,1)} %fusion.1.q_ref.k_ref.v_ref, bf16[1,1024,3456]{2,1,0:T(8,128)(2,1)} %fusion.1.q_ref.k_ref.v_ref, bf16[1,1024,1152]{2,1,0:T(8,128)(2,1)} %fusion.25.g_ref, ...), custom_call_target="tpu_custom_call" | custom-call | flops 42949672 | bytes 18874 | tf_op jit(solution)/shard_map/pallas_call | solution.py:241
  619.6 6.8 convolution_convert_fusion.2
  633.9 9.1 %add_convert_fusion.2 = bf16[1152,1792]{1,0:T(8,128)(2,1)S(1)} fusion(bf16[1152,1792]{1,0:T(8,128)(2,1)} %collective-permute-done.55, pred[]{:T(512)S(6)} %eq.80, bf16[1024,3456]{1,0:T(8,128)(2,1)} %bitcast.357, bf16[1,1024,1152]{2,1,0:T(8,128)(2,1)S(1)} %copy-done.56), kind=kOutput, calls=%fused_computation.6 | convolution fusion | flops 4235886592 | bytes 17956864 | tf_op jit(solution)/shard_map/dot_general | solution.py:51
  644.5 9.6 %collective-permute-done.56 = bf16[4,72,1792]{2,1,0:T(8,128)(2,1)S(1)} collective-permute-done((bf16[4,72,1792]{2,1,0:T(8,128)(2,1)S(1)}, bf16[4,72,1792]{2,1,0:T(8,128)(2,1)S(1)}, u32[]{:S(2)}, u32[]{:S(2)}) %collective-permute-start.56) | collective-permute-done | bytes 1032224 | tf_op jit(solution)/shard_map/ppermute | solution.py:850
  666.5 20.9 %shard_map.227 = (f32[1,1024,1152]{2,1,0:T(8,128)}, f32[1,1,1152]{2,1,0:T(1,128)}, f32[1,1,1152]{2,1,0:T(1,128)}, f32[1,1,3456]{2,1,0:T(1,128)}) custom-call(bf16[1,1024,3456]{2,1,0:T(8,128)(2,1)} %shard_map.226, bf16[1152,3456]{1,0:T(8,128)(2,1)} %bitcast.356, bf16[1,1024,1152]{2,1,0:T(8,128)(2,1)} %copy-done, f32[1,1,1152]{2,1,0:T(1,128)} %get-tuple-element.390.scale_ref, ...), custom_call_target="tpu_custom_call" | custom-call | flops 8153726 | bytes 26836 | tf_op jit(solution)/shard_map/pallas_call | solution.py:582
  695.0 7.6 collective-permute-done.70
  743.1 10.9 %collective-permute-done.75 = bf16[72,1792]{1,0:T(8,128)(2,1)} collective-permute-done((bf16[72,1792]{1,0:T(8,128)(2,1)}, bf16[72,1792]{1,0:T(8,128)(2,1)}, u32[]{:S(2)}, u32[]{:S(2)}) %collective-permute-start.75) | collective-permute-done | bytes 258080 | tf_op jit(solution)/shard_map/ppermute | solution.py:876
  (531 shorter events, 281.9 us)
Async XLA Ops:
  7.2 274.7 %all-gather.2.cloned.1.call-start = ((), (), s32[]{:S(2)}) async-start(), calls=%async_computation | async-start | bytes 11280384 | tf_op jit(solution)/shard_map/all_gather | solution.py:994
  23.0 35.1 %collective-permute-start.1 = (bf16[72,1728]{1,0:T(8,128)(2,1)S(1)}, bf16[72,1728]{1,0:T(8,128)(2,1)S(1)}, u32[]{:S(2)}, u32[]{:S(2)}) collective-permute-start(bf16[72,1728]{1,0:T(8,128)(2,1)S(1)} %copy-done.17), channel_id=1, source_target_pairs={{0,16},{2,18},{4,20},{6,22},{8,24},{10,26},{12,28},{14,30},{16,0},... | collective-permute-start | bytes 746504 | tf_op jit(solution)/shard_map/ppermute | solution.py:719
  23.1 35.1 %collective-permute-start.2 = (bf16[72,1728]{1,0:T(8,128)(2,1)S(1)}, bf16[72,1728]{1,0:T(8,128)(2,1)S(1)}, u32[]{:S(2)}, u32[]{:S(2)}) collective-permute-start(bf16[72,1728]{1,0:T(8,128)(2,1)S(1)} %copy-done.17), channel_id=1, source_target_pairs={{0,8},{2,10},{4,12},{6,14},{8,16},{10,18},{12,20},{14,22},{16,24},... | collective-permute-start | bytes 746504 | tf_op jit(solution)/shard_map/ppermute | solution.py:719
  26.8 46.8 %collective-permute-start.10 = (bf16[1,512,1152]{2,1,0:T(8,128)(2,1)S(1)}, bf16[1,512,1152]{2,1,0:T(8,128)(2,1)S(1)}, u32[]{:S(2)}, u32[]{:S(2)}) collective-permute-start(bf16[1,512,1152]{2,1,0:T(8,128)(2,1)S(1)} %get-tuple-element.343), channel_id=1, source_target_pairs={{0,1},{1,0},{2,3},{3,2},{4,5},{5,4},{6,7},{7,6},{8,9},{9,8},{10,11... | collective-permute-start | bytes 3538952 | tf_op jit(solution)/shard_map/ppermute | solution.py:907
  33.5 30.8 %collective-permute-start.7 = (bf16[2,2,72,128]{3,2,1,0:T(8,128)(2,1)S(1)}, bf16[2,2,72,128]{3,2,1,0:T(8,128)(2,1)S(1)}, u32[]{:S(2)}, u32[]{:S(2)}) collective-permute-start(bf16[2,2,72,128]{3,2,1,0:T(8,128)(2,1)S(1)} %get-tuple-element.316), channel_id=1, source_target_pairs={{0,24},{2,26},{4,28},{6,30},{8,0},{10,2},{12,4},{14,6},{16,8},{18,... | collective-permute-start | bytes 221192 | tf_op jit(solution)/shard_map/ppermute | solution.py:824
  36.3 36.6 %collective-permute-start.11 = (bf16[1,60,1152]{2,1,0:T(8,128)(2,1)S(1)}, bf16[1,60,1152]{2,1,0:T(8,128)(2,1)S(1)}, u32[]{:S(2)}, u32[]{:S(2)}) collective-permute-start(bf16[1,60,1152]{2,1,0:T(8,128)(2,1)S(1)} %get-tuple-element.378), channel_id=1, source_target_pairs={{0,1},{1,0},{2,3},{3,2},{4,5},{5,4},{6,7},{7,6},{8,9},{9,8},{10,11... | collective-permute-start | bytes 414728 | tf_op jit(solution)/shard_map/ppermute | solution.py:907
  77.1 33.2 %collective-permute-start.14 = (bf16[4,72,1728]{2,1,0:T(8,128)(2,1)S(1)}, bf16[4,72,1728]{2,1,0:T(8,128)(2,1)}, u32[]{:S(2)}, u32[]{:S(2)}) collective-permute-start(bf16[4,72,1728]{2,1,0:T(8,128)(2,1)S(1)} %shard_map.211.refs_0_), channel_id=1, source_target_pairs={{0,2},{2,0},{4,6},{6,4},{8,10},{10,8},{12,14},{14,12},{16,18},{18,... | collective-permute-start | bytes 2985992 | tf_op jit(solution)/shard_map/ppermute | solution.py:733
  80.5 34.5 %collective-permute-start.17 = (bf16[72,2880]{1,0:T(8,128)(2,1)}, bf16[72,2880]{1,0:T(8,128)(2,1)}, u32[]{:S(2)}, u32[]{:S(2)}) collective-permute-start(bf16[72,2880]{1,0:T(8,128)(2,1)} %concatenate.122.refs_0_), channel_id=1, source_target_pairs={{0,24},{2,26},{4,28},{6,30},{8,0},{10,2},{12,4},{14,6},{16,8},{18,... | collective-permute-start | bytes 1244168 | tf_op jit(solution)/shard_map/ppermute | solution.py:719
  80.5 53.6 %collective-permute-start.18 = (bf16[72,2880]{1,0:T(8,128)(2,1)}, bf16[72,2880]{1,0:T(8,128)(2,1)}, u32[]{:S(2)}, u32[]{:S(2)}) collective-permute-start(bf16[72,2880]{1,0:T(8,128)(2,1)} %concatenate.122.refs_0_), channel_id=1, source_target_pairs={{0,16},{2,18},{4,20},{6,22},{8,24},{10,26},{12,28},{14,30},{16,0},... | collective-permute-start | bytes 1244168 | tf_op jit(solution)/shard_map/ppermute | solution.py:719
  82.3 51.9 %collective-permute-start.19 = (bf16[72,2880]{1,0:T(8,128)(2,1)}, bf16[72,2880]{1,0:T(8,128)(2,1)}, u32[]{:S(2)}, u32[]{:S(2)}) collective-permute-start(bf16[72,2880]{1,0:T(8,128)(2,1)} %concatenate.122.refs_0_), channel_id=1, source_target_pairs={{0,8},{2,10},{4,12},{6,14},{8,16},{10,18},{12,20},{14,22},{16,24},... | collective-permute-start | bytes 1244168 | tf_op jit(solution)/shard_map/ppermute | solution.py:719
  100.3 36.2 %collective-permute-start.15 = (bf16[4,72,896]{2,1,0:T(8,128)(2,1)S(1)}, bf16[4,72,896]{2,1,0:T(8,128)(2,1)S(1)}, u32[]{:S(2)}, u32[]{:S(2)}) collective-permute-start(bf16[4,72,896]{2,1,0:T(8,128)(2,1)S(1)} %slice.292), channel_id=1, source_target_pairs={{0,2},{2,0},{4,6},{6,4},{8,10},{10,8},{12,14},{14,12},{16,18},{18,... | collective-permute-start | bytes 1548296 | tf_op jit(solution)/shard_map/ppermute | solution.py:740
  140.0 71.2 %collective-permute-start.25 = (bf16[4,72,2880]{2,1,0:T(8,128)(2,1)S(1)}, bf16[4,72,2880]{2,1,0:T(8,128)(2,1)S(1)}, u32[]{:S(2)}, u32[]{:S(2)}) collective-permute-start(bf16[4,72,2880]{2,1,0:T(8,128)(2,1)S(1)} %shard_map.212.refs_0_), channel_id=1, source_target_pairs={{0,4},{2,6},{4,0},{6,2},{8,12},{10,14},{12,8},{14,10},{16,20},{18,... | collective-permute-start | bytes 4976648 | tf_op jit(solution)/shard_map/ppermute | solution.py:732
  141.2 69.9 %collective-permute-start.26 = (bf16[4,72,2880]{2,1,0:T(8,128)(2,1)S(1)}, bf16[4,72,2880]{2,1,0:T(8,128)(2,1)S(1)}, u32[]{:S(2)}, u32[]{:S(2)}) collective-permute-start(bf16[4,72,2880]{2,1,0:T(8,128)(2,1)S(1)} %shard_map.212.refs_0_), channel_id=1, source_target_pairs={{0,2},{2,0},{4,6},{6,4},{8,10},{10,8},{12,14},{14,12},{16,18},{18,... | collective-permute-start | bytes 4976648 | tf_op jit(solution)/shard_map/ppermute | solution.py:733
  381.4 31.5 %collective-permute-start.37 = (bf16[4,2,72,1152]{3,2,0,1:T(8,128)(2,1)}, bf16[4,2,72,1152]{3,2,0,1:T(8,128)(2,1)}, u32[]{:S(2)}, u32[]{:S(2)}) collective-permute-start(bf16[4,2,72,1152]{3,2,0,1:T(8,128)(2,1)} %bitcast.334), channel_id=1, source_target_pairs={{0,2},{2,0},{4,6},{6,4},{8,10},{10,8},{12,14},{14,12},{16,18},{18,... | collective-permute-start | bytes 3981320 | tf_op jit(solution)/shard_map/ppermute | solution.py:850
  382.9 32.6 %collective-permute-start.38 = (bf16[4,2,72,1152]{3,2,0,1:T(8,128)(2,1)}, bf16[4,2,72,1152]{3,2,0,1:T(8,128)(2,1)}, u32[]{:S(2)}, u32[]{:S(2)}) collective-permute-start(bf16[4,2,72,1152]{3,2,0,1:T(8,128)(2,1)} %bitcast.333), channel_id=1, source_target_pairs={{0,4},{2,6},{4,0},{6,2},{8,12},{10,14},{12,8},{14,10},{16,20},{18,... | collective-permute-start | bytes 3981320 | tf_op jit(solution)/shard_map/ppermute | solution.py:850
  418.5 30.4 %collective-permute-start.40 = (bf16[4,2,72,1152]{3,2,0,1:T(8,128)(2,1)S(1)}, bf16[4,2,72,1152]{3,2,0,1:T(8,128)(2,1)}, u32[]{:S(2)}, u32[]{:S(2)}) collective-permute-start(bf16[4,2,72,1152]{3,2,0,1:T(8,128)(2,1)S(1)} %bitcast.398), channel_id=1, source_target_pairs={{0,2},{2,0},{4,6},{6,4},{8,10},{10,8},{12,14},{14,12},{16,18},{18,... | collective-permute-start | bytes 3981320 | tf_op jit(solution)/shard_map/ppermute | solution.py:850
  420.0 31.5 %collective-permute-start.41 = (bf16[4,2,72,1152]{3,2,0,1:T(8,128)(2,1)S(1)}, bf16[4,2,72,1152]{3,2,0,1:T(8,128)(2,1)S(1)}, u32[]{:S(2)}, u32[]{:S(2)}) collective-permute-start(bf16[4,2,72,1152]{3,2,0,1:T(8,128)(2,1)S(1)} %bitcast.397), channel_id=1, source_target_pairs={{0,4},{2,6},{4,0},{6,2},{8,12},{10,14},{12,8},{14,10},{16,20},{18,... | collective-permute-start | bytes 3981320 | tf_op jit(solution)/shard_map/ppermute | solution.py:850
  457.9 35.4 %collective-permute-start.46 = (bf16[4,72,1152]{2,1,0:T(8,128)(2,1)}, bf16[4,72,1152]{2,1,0:T(8,128)(2,1)}, u32[]{:S(2)}, u32[]{:S(2)}) collective-permute-start(bf16[4,72,1152]{2,1,0:T(8,128)(2,1)} %dynamic-slice_bitcast_fusion.7), channel_id=1, source_target_pairs={{0,2},{2,0},{4,6},{6,4},{8,10},{10,8},{12,14},{14,12},{16,18},{18,... | collective-permute-start | bytes 1990664 | tf_op jit(solution)/shard_map/ppermute | solution.py:850
  459.5 33.9 %collective-permute-start.45 = (bf16[4,72,1152]{2,1,0:T(8,128)(2,1)}, bf16[4,72,1152]{2,1,0:T(8,128)(2,1)S(1)}, u32[]{:S(2)}, u32[]{:S(2)}) collective-permute-start(bf16[4,72,1152]{2,1,0:T(8,128)(2,1)} %dynamic-slice_bitcast_fusion.8), channel_id=1, source_target_pairs={{0,4},{2,6},{4,0},{6,2},{8,12},{10,14},{12,8},{14,10},{16,20},{18,... | collective-permute-start | bytes 1990664 | tf_op jit(solution)/shard_map/ppermute | solution.py:850
  460.0 33.3 %collective-permute-start.44 = (bf16[4,72,1152]{2,1,0:T(8,128)(2,1)}, bf16[4,72,1152]{2,1,0:T(8,128)(2,1)}, u32[]{:S(2)}, u32[]{:S(2)}) collective-permute-start(bf16[4,72,1152]{2,1,0:T(8,128)(2,1)} %dynamic-slice_bitcast_fusion.5), channel_id=1, source_target_pairs={{0,2},{2,0},{4,6},{6,4},{8,10},{10,8},{12,14},{14,12},{16,18},{18,... | collective-permute-start | bytes 1990664 | tf_op jit(solution)/shard_map/ppermute | solution.py:850
  461.4 32.8 %collective-permute-start.42 = (bf16[4,72,1152]{2,1,0:T(8,128)(2,1)}, bf16[4,72,1152]{2,1,0:T(8,128)(2,1)}, u32[]{:S(2)}, u32[]{:S(2)}) collective-permute-start(bf16[4,72,1152]{2,1,0:T(8,128)(2,1)} %dynamic-slice_bitcast_fusion.6), channel_id=1, source_target_pairs={{0,4},{2,6},{4,0},{6,2},{8,12},{10,14},{12,8},{14,10},{16,20},{18,... | collective-permute-start | bytes 1990664 | tf_op jit(solution)/shard_map/ppermute | solution.py:850
  515.7 94.4 %collective-permute-start.54 = (bf16[72,4608]{1,0:T(8,128)(2,1)}, bf16[72,4608]{1,0:T(8,128)(2,1)}, u32[]{:S(2)}, u32[]{:S(2)}) collective-permute-start(bf16[72,4608]{1,0:T(8,128)(2,1)} %get-tuple-element.233), channel_id=1, source_target_pairs={{0,24},{2,26},{4,28},{6,30},{8,0},{10,2},{12,4},{14,6},{16,8},{18,... | collective-permute-start | bytes 1990664 | tf_op jit(solution)/shard_map/ppermute | solution.py:876
  515.8 94.3 %collective-permute-start.53 = (bf16[72,4608]{1,0:T(8,128)(2,1)}, bf16[72,4608]{1,0:T(8,128)(2,1)}, u32[]{:S(2)}, u32[]{:S(2)}) collective-permute-start(bf16[72,4608]{1,0:T(8,128)(2,1)} %get-tuple-element.231), channel_id=1, source_target_pairs={{0,16},{2,18},{4,20},{6,22},{8,24},{10,26},{12,28},{14,30},{16,0},... | collective-permute-start | bytes 1990664 | tf_op jit(solution)/shard_map/ppermute | solution.py:876
  529.2 80.9 %collective-permute-start.52 = (bf16[72,4608]{1,0:T(8,128)(2,1)}, bf16[72,4608]{1,0:T(8,128)(2,1)}, u32[]{:S(2)}, u32[]{:S(2)}) collective-permute-start(bf16[72,4608]{1,0:T(8,128)(2,1)} %get-tuple-element.229), channel_id=1, source_target_pairs={{0,8},{2,10},{4,12},{6,14},{8,16},{10,18},{12,20},{14,22},{16,24},... | collective-permute-start | bytes 1990664 | tf_op jit(solution)/shard_map/ppermute | solution.py:876
  542.3 70.8 %collective-permute-start.51 = (bf16[4,2,72,1280]{3,2,0,1:T(8,128)(2,1)}, bf16[4,2,72,1280]{3,2,0,1:T(8,128)(2,1)}, u32[]{:S(2)}, u32[]{:S(2)}) collective-permute-start(bf16[4,2,72,1280]{3,2,0,1:T(8,128)(2,1)} %pad_maximum_fusion.4), channel_id=1, source_target_pairs={{0,4},{2,6},{4,0},{6,2},{8,12},{10,14},{12,8},{14,10},{16,20},{18,... | collective-permute-start | bytes 4423688 | tf_op jit(solution)/shard_map/ppermute | solution.py:850
  543.7 72.3 %collective-permute-start.50 = (bf16[4,2,72,1792]{3,2,0,1:T(8,128)(2,1)}, bf16[4,2,72,1792]{3,2,0,1:T(8,128)(2,1)}, u32[]{:S(2)}, u32[]{:S(2)}) collective-permute-start(bf16[4,2,72,1792]{3,2,0,1:T(8,128)(2,1)} %pad_maximum_fusion.3), channel_id=1, source_target_pairs={{0,2},{2,0},{4,6},{6,4},{8,10},{10,8},{12,14},{14,12},{16,18},{18,... | collective-permute-start | bytes 6193160 | tf_op jit(solution)/shard_map/ppermute | solution.py:850
  628.7 32.2 %collective-permute-start.39 = (bf16[1,512,1152]{2,1,0:T(8,128)(2,1)S(1)}, bf16[1,512,1152]{2,1,0:T(8,128)(2,1)S(1)}, u32[]{:S(2)}, u32[]{:S(2)}) collective-permute-start(bf16[1,512,1152]{2,1,0:T(8,128)(2,1)S(1)} %get-tuple-element.339), channel_id=1, source_target_pairs={{0,1},{1,0},{2,3},{3,2},{4,5},{5,4},{6,7},{7,6},{8,9},{9,8},{10,11... | collective-permute-start | bytes 3538952 | tf_op jit(solution)/shard_map/ppermute | solution.py:921
  658.4 29.0 %collective-permute-start.58 = (bf16[4,2,72,896]{3,2,0,1:T(8,128)(2,1)}, bf16[4,2,72,896]{3,2,0,1:T(8,128)(2,1)S(1)}, u32[]{:S(2)}, u32[]{:S(2)}) collective-permute-start(bf16[4,2,72,896]{3,2,0,1:T(8,128)(2,1)} %bitcast.336), channel_id=1, source_target_pairs={{0,2},{2,0},{4,6},{6,4},{8,10},{10,8},{12,14},{14,12},{16,18},{18,... | collective-permute-start | bytes 3096584 | tf_op jit(solution)/shard_map/ppermute | solution.py:850
  663.7 29.9 %collective-permute-start.71 = (bf16[72,3072]{1,0:T(8,128)(2,1)}, bf16[72,3072]{1,0:T(8,128)(2,1)}, u32[]{:S(2)}, u32[]{:S(2)}) collective-permute-start(bf16[72,3072]{1,0:T(8,128)(2,1)} %get-tuple-element.277), channel_id=1, source_target_pairs={{0,24},{2,26},{4,28},{6,30},{8,0},{10,2},{12,4},{14,6},{16,8},{18,... | collective-permute-start | bytes 1327112 | tf_op jit(solution)/shard_map/ppermute | solution.py:876
  665.8 36.8 %collective-permute-start.70 = (bf16[72,3072]{1,0:T(8,128)(2,1)}, bf16[72,3072]{1,0:T(8,128)(2,1)}, u32[]{:S(2)}, u32[]{:S(2)}) collective-permute-start(bf16[72,3072]{1,0:T(8,128)(2,1)} %get-tuple-element.275), channel_id=1, source_target_pairs={{0,16},{2,18},{4,20},{6,22},{8,24},{10,26},{12,28},{14,30},{16,0},... | collective-permute-start | bytes 1327112 | tf_op jit(solution)/shard_map/ppermute | solution.py:876
  665.8 40.8 %collective-permute-start.69 = (bf16[72,3072]{1,0:T(8,128)(2,1)}, bf16[72,3072]{1,0:T(8,128)(2,1)}, u32[]{:S(2)}, u32[]{:S(2)}) collective-permute-start(bf16[72,3072]{1,0:T(8,128)(2,1)} %get-tuple-element.273), channel_id=1, source_target_pairs={{0,8},{2,10},{4,12},{6,14},{8,16},{10,18},{12,20},{14,22},{16,24},... | collective-permute-start | bytes 1327112 | tf_op jit(solution)/shard_map/ppermute | solution.py:876
  693.6 30.4 %collective-permute-start.62 = (bf16[4,72,896]{2,1,0:T(8,128)(2,1)}, bf16[4,72,896]{2,1,0:T(8,128)(2,1)}, u32[]{:S(2)}, u32[]{:S(2)}) collective-permute-start(bf16[4,72,896]{2,1,0:T(8,128)(2,1)} %dynamic-slice_bitcast_fusion.10), channel_id=1, source_target_pairs={{0,4},{2,6},{4,0},{6,2},{8,12},{10,14},{12,8},{14,10},{16,20},{18,... | collective-permute-start | bytes 1548296 | tf_op jit(solution)/shard_map/ppermute | solution.py:850
  (144 other events, 1661.1 us)
Sparse Core Ops, SparseCore 0:
  18.3 213.7 all-gather.1
